TPU v7x, 32 devices: a whole 2x2x4 slice. The times are simulated.
32 devices in a mesh: dp: 32 (over z, y, x, core).
Axes of the slice: x: 2, y: 2, z: 4, core: 2. Of those that a mesh axis runs over, the one named last changes fastest.
Arguments:
- tokens: bfloat16 [16384, 1024], P('dp'), may hold values from -6 to 6
- query_weight: bfloat16 [1024, 1024], P('dp'), may hold values from -0.375 to 0.375
- key_projection_weight: bfloat16 [1024, 512], P('dp'), may hold values from -0.1875 to 0.1875
- value_projection_weight: bfloat16 [1024, 512], P('dp'), may hold values from -0.1875 to 0.1875
- output_weight: bfloat16 [1024, 1024], P(None, 'dp'), may hold values from -1.5 to 1.5
- first_gain: bfloat16 [1024], P('dp'), may hold values from 0.5 to 1.5
- second_gain: bfloat16 [1024], P('dp'), may hold values from 0.5 to 1.5
- router_weight: bfloat16 [1024, 16], P('dp'), may hold values from -0.09375 to 0.09375
- gate_weight: bfloat16 [16, 1024, 512], P(None, 'dp'), may hold values from -0.1875 to 0.1875
- up_weight: bfloat16 [16, 1024, 512], P(None, 'dp'), may hold values from -0.1875 to 0.1875
- down_weight: bfloat16 [16, 512, 1024], P(None, None, 'dp'), may hold values from -0.75 to 0.75
- routes: int32 [16384, 8], P('dp'), may hold values from 0 to 15, all different within a row; in each aligned block of 512 rows (0 to 511, 512 to 1023, ...) at most 288 rows name the same one
- segments: int32 [32, 512], P('dp'), may hold values from 0 to 7, never falling along the last dimension, each value on 1 to 256 neighbouring positions
- cotangent: bfloat16 [16384, 1024], P('dp'), may hold values from -6 to 6
Outputs:
- output: bfloat16 [16384, 1024], P('dp')
- input_grad: float32 [16384, 1024], P('dp')
- query_grad: float32 [1024, 1024], P('dp')
- key_grad: float32 [1024, 512], P('dp')
- value_grad: float32 [1024, 512], P('dp')
- output_weight_grad: float32 [1024, 1024], P(None, 'dp')
- first_gain_grad: float32 [1024], P('dp')
- second_gain_grad: float32 [1024], P('dp')
- router_grad: float32 [1024, 16], P('dp')
- gate_grad: float32 [16, 1024, 512], P(None, 'dp')
- up_grad: float32 [16, 1024, 512], P(None, 'dp')
- down_grad: float32 [16, 512, 1024], P(None, None, 'dp')
Inputs may be any that keep to these rules, and one draw needn't show every extreme that they name: `routes`: each token names 8 different experts; the 512 tokens of one device name no expert more than 288 times, a bound that some block reaches. `segments`: along each sequence the document numbers never fall; each document has 1 to 256 tokens, one exactly 256.
All inputs are finite; a program needn't handle non-finite values.
Results may differ from a plain program's by a relative error of at most 0.013.
The roundings to bfloat16 on the way count: a program that leaves them out, or rounds other values in their place, can miss the bound.
Values may be sent and summed in bfloat16 or wider, within the bound.
No kernel may reach another device: no remote copies, remote signals or barrier semaphores. Data moves between devices by JAX's collectives and lax.ppermute only.
A program may use at most 320 MiB of HBM per device.

v0:
```python
import math

import jax
import jax.numpy as jnp
from jax import lax
from jax.sharding import PartitionSpec as P

QUERY_HEADS = 16
KEY_VALUE_HEADS = 8
HEAD_SIZE = 64
EXPERTS = 16
CAP = 288


epsilon = 1e-06
neg_large = -1000000000.0


def rms_scale(values):
    return lax.rsqrt(jnp.mean(values * values, axis=-1, keepdims=True) + epsilon)


def norm_back(values, scale_rows, gain_full, grad_out):
    weighted = grad_out * gain_full
    gain_grad = jnp.sum(grad_out * values * scale_rows, axis=0)
    inner_mean = jnp.mean(weighted * values, axis=-1, keepdims=True)
    grad_in = scale_rows * weighted - values * (scale_rows * scale_rows * scale_rows) * inner_mean
    return (grad_in, gain_grad)


def rope_tables(sequence_length, head_dim, copies):
    positions = jnp.arange(sequence_length, dtype=jnp.float32)
    frequency = 10000.0 ** (-2.0 * jnp.arange(head_dim // 2, dtype=jnp.float32) / head_dim)
    angles = jnp.tile(positions[:, None] * frequency[None, :], (copies, 1))
    return (jnp.cos(angles), jnp.sin(angles))


def rotate(values, cosine_lookup, sine_lookup):
    half_dim = values.shape[-1] // 2
    first_half = values[..., :half_dim]
    second_half = values[..., half_dim:]
    cos_part = cosine_lookup[:, None, :]
    sin_part = sine_lookup[:, None, :]
    return jnp.concatenate(
        [
            first_half * cos_part - second_half * sin_part,
            second_half * cos_part + first_half * sin_part,
        ],
        axis=-1,
    )


def inverse_rotation(grads, cosine_lookup, sine_lookup):
    half_dim = grads.shape[-1] // 2
    first_half = grads[..., :half_dim]
    second_half = grads[..., half_dim:]
    cos_part = cosine_lookup[:, None, :]
    sin_part = sine_lookup[:, None, :]
    return jnp.concatenate(
        [
            first_half * cos_part + second_half * sin_part,
            second_half * cos_part - first_half * sin_part,
        ],
        axis=-1,
    )


def slot_tables(routes, experts, capacity):
    number_of_rows, picks = routes.shape
    flat_routes = routes.reshape(-1)
    one_hot = (flat_routes[:, None] == jnp.arange(experts, dtype=jnp.int32)[None, :]).astype(
        jnp.int32
    )
    slot_rank = jnp.sum((jnp.cumsum(one_hot, axis=0) - 1) * one_hot, axis=1)
    slot_index = flat_routes * capacity + slot_rank
    owners = (
        jnp.zeros((experts * capacity,), jnp.int32)
        .at[slot_index]
        .set(jnp.arange(number_of_rows * picks, dtype=jnp.int32) // picks)
    )
    filled = jnp.zeros((experts * capacity,), jnp.int32).at[slot_index].set(1)
    return (slot_index.reshape(number_of_rows, picks), owners, filled)


def block_forward(query_blk, key_part, value_part, allowed, score_scale):
    raw_scores = jnp.einsum(
        "qgrd,kgd->grqk", query_blk, key_part, preferred_element_type=jnp.float32
    )
    scores = jnp.where(allowed, raw_scores * score_scale, neg_large)
    largest = jnp.max(scores, axis=-1, keepdims=True)
    exponent = jnp.exp(scores - largest)
    totals = jnp.sum(exponent, axis=-1, keepdims=True)
    prob_low = (exponent / totals).astype(jnp.bfloat16)
    mixed_heads = jnp.einsum(
        "grqk,kgd->qgrd", prob_low, value_part, preferred_element_type=jnp.float32
    )
    return (mixed_heads, (largest + jnp.log(totals))[..., 0])


def block_backward(query_blk, key_part, value_part, allowed, log_total, grad_blk, score_scale):
    raw_scores = jnp.einsum(
        "qgrd,kgd->grqk", query_blk, key_part, preferred_element_type=jnp.float32
    )
    scores = jnp.where(allowed, raw_scores * score_scale, neg_large)
    prob_full = jnp.exp(scores - log_total[..., None])
    grad_probs = jnp.einsum(
        "qgrd,kgd->grqk", grad_blk, value_part, preferred_element_type=jnp.float32
    )
    inner_sum = jnp.sum(prob_full * grad_probs, axis=-1, keepdims=True)
    grad_scores = (prob_full * (grad_probs - inner_sum)).astype(jnp.bfloat16)
    grad_query = (
        jnp.einsum("grqk,kgd->qgrd", grad_scores, key_part, preferred_element_type=jnp.float32)
        * score_scale
    )
    grad_key = (
        jnp.einsum("grqk,qgrd->kgd", grad_scores, query_blk, preferred_element_type=jnp.float32)
        * score_scale
    )
    value_gradient_rows = jnp.einsum(
        "grqk,qgrd->kgd",
        prob_full.astype(jnp.bfloat16),
        grad_blk,
        preferred_element_type=jnp.float32,
    )
    return (grad_query, grad_key, value_gradient_rows)


def allowed_table(seg_seq, begin_row, end_row):
    positions = jnp.arange(end_row, dtype=jnp.int32)
    same_doc = seg_seq[begin_row:end_row, None] == seg_seq[None, :end_row]
    causal = positions[begin_row:end_row, None] >= positions[None, :]
    return same_doc & causal


def sequence_forward(packed):
    query_sequence, key_seq, value_seq, seg_seq = packed
    sequence_length = seg_seq.shape[0]
    rows_per_block = min(512, sequence_length)
    score_scale = 1.0 / math.sqrt(query_sequence.shape[-1])
    allowed = allowed_table(seg_seq, 0, rows_per_block)
    mixed_heads, log_total = block_forward(query_sequence, key_seq, value_seq, allowed, score_scale)
    pieces = [mixed_heads]
    log_totals = [log_total]
    return (jnp.concatenate(pieces, axis=0), jnp.stack(log_totals, axis=0))


def sequence_backward(packed):
    query_sequence, key_seq, value_seq, seg_seq, log_seq, grad_seq = packed
    sequence_length = seg_seq.shape[0]
    rows_per_block = min(512, sequence_length)
    score_scale = 1.0 / math.sqrt(query_sequence.shape[-1])
    query_grads = []
    key_total = jnp.zeros(key_seq.shape, jnp.float32)
    value_total = jnp.zeros(value_seq.shape, jnp.float32)
    for block_number, begin_row in enumerate(range(0, sequence_length, rows_per_block)):
        end_row = begin_row + rows_per_block
        allowed = allowed_table(seg_seq, begin_row, end_row)
        grad_query, grad_key, value_gradient_rows = block_backward(
            query_sequence,
            key_seq,
            value_seq,
            allowed,
            log_seq[block_number],
            grad_seq,
            score_scale,
        )
        query_grads.append(grad_query)
        key_total = key_total.at[:end_row].add(grad_key)
        value_total = value_total.at[:end_row].add(value_gradient_rows)
    return (jnp.concatenate(query_grads, axis=0), key_total, value_total)


def local(
    tokens,
    query_weight,
    key_projection_weight,
    value_projection_weight,
    output_weight,
    first_gain,
    second_gain,
    router_weight,
    gate_weight,
    up_weight,
    down_weight,
    routes,
    segments,
    cotangent,
):
    dense_full = (
        lax.all_gather(query_weight, "dp", axis=0, tiled=True),
        lax.all_gather(key_projection_weight, "dp", axis=0, tiled=True),
        lax.all_gather(value_projection_weight, "dp", axis=0, tiled=True),
        lax.all_gather(output_weight, "dp", axis=1, tiled=True),
        lax.all_gather(first_gain, "dp", axis=0, tiled=True),
        lax.all_gather(second_gain, "dp", axis=0, tiled=True),
        lax.all_gather(router_weight, "dp", axis=0, tiled=True),
    )
    expert_full = (
        lax.all_gather(gate_weight, "dp", axis=1, tiled=True),
        lax.all_gather(up_weight, "dp", axis=1, tiled=True),
        lax.all_gather(down_weight, "dp", axis=2, tiled=True),
    )
    query_full, key_full, value_full, output_full, gain_one, gain_two, router_full = dense_full
    gate_full, up_full, down_full = expert_full
    number_of_rows, width = tokens.shape
    sequence_count, sequence_length = segments.shape
    query_group_width = QUERY_HEADS // KEY_VALUE_HEADS
    cosine_lookup, sine_lookup = rope_tables(sequence_length, HEAD_SIZE, sequence_count)
    inputs = tokens.astype(jnp.float32)
    first_scale = rms_scale(inputs)
    first_normed_input = (inputs * first_scale * gain_one.astype(jnp.float32)).astype(jnp.bfloat16)
    query_proj = jnp.dot(
        first_normed_input, query_full, preferred_element_type=jnp.float32
    ).reshape(number_of_rows, QUERY_HEADS, HEAD_SIZE)
    key_proj = jnp.dot(first_normed_input, key_full, preferred_element_type=jnp.float32).reshape(
        number_of_rows, KEY_VALUE_HEADS, HEAD_SIZE
    )
    query_rotated = rotate(query_proj, cosine_lookup, sine_lookup).astype(jnp.bfloat16)
    key_rotated = rotate(key_proj, cosine_lookup, sine_lookup).astype(jnp.bfloat16)
    value_reduced_precision = jnp.dot(
        first_normed_input, value_full, preferred_element_type=jnp.float32
    ).astype(jnp.bfloat16)
    query_sequences = query_rotated.reshape(
        sequence_count, sequence_length, KEY_VALUE_HEADS, query_group_width, HEAD_SIZE
    )
    key_sequences = key_rotated.reshape(sequence_count, sequence_length, KEY_VALUE_HEADS, HEAD_SIZE)
    value_sequences = value_reduced_precision.reshape(
        sequence_count, sequence_length, KEY_VALUE_HEADS, HEAD_SIZE
    )
    mixed_heads, log_totals = lax.map(
        sequence_forward, (query_sequences, key_sequences, value_sequences, segments)
    )
    attn_low = mixed_heads.reshape(number_of_rows, QUERY_HEADS * HEAD_SIZE).astype(jnp.bfloat16)
    resid = inputs + jnp.dot(attn_low, output_full, preferred_element_type=jnp.float32)
    second_scale = rms_scale(resid)
    normed_two = (resid * second_scale * gain_two.astype(jnp.float32)).astype(jnp.bfloat16)
    logits = jnp.dot(normed_two, router_full, preferred_element_type=jnp.float32)
    route_hot = (routes[:, :, None] == jnp.arange(EXPERTS, dtype=jnp.int32)[None, None, :]).astype(
        jnp.float32
    )
    chosen = jnp.sum(logits[:, None, :] * route_hot, axis=-1)
    gates = jax.nn.softmax(chosen, axis=-1)
    slot_index, owners, filled = slot_tables(routes, EXPERTS, CAP)
    gathered = jnp.where(
        filled[:, None] > 0, normed_two[owners], jnp.zeros((), jnp.bfloat16)
    ).reshape(EXPERTS, CAP, width)
    gate_act = jnp.einsum("ecd,edf->ecf", gathered, gate_full, preferred_element_type=jnp.float32)
    up_act = jnp.einsum("ecd,edf->ecf", gathered, up_full, preferred_element_type=jnp.float32)
    sigmoid_gate = jax.nn.sigmoid(gate_act)
    silu_gate = gate_act * sigmoid_gate
    hidden = (silu_gate * up_act).astype(jnp.bfloat16)
    expert_out = jnp.einsum(
        "ecf,efd->ecd", hidden, down_full, preferred_element_type=jnp.float32
    ).reshape(EXPERTS * CAP, width)
    picked = expert_out[slot_index]
    output = (resid + jnp.sum(gates[:, :, None] * picked, axis=1)).astype(jnp.bfloat16)
    dense_back = (
        lax.all_gather(query_weight, "dp", axis=0, tiled=True),
        lax.all_gather(key_projection_weight, "dp", axis=0, tiled=True),
        lax.all_gather(value_projection_weight, "dp", axis=0, tiled=True),
        lax.all_gather(output_weight, "dp", axis=1, tiled=True),
        lax.all_gather(first_gain, "dp", axis=0, tiled=True),
        lax.all_gather(second_gain, "dp", axis=0, tiled=True),
        lax.all_gather(router_weight, "dp", axis=0, tiled=True),
    )
    expert_back = (
        lax.all_gather(gate_weight, "dp", axis=1, tiled=True),
        lax.all_gather(up_weight, "dp", axis=1, tiled=True),
        lax.all_gather(down_weight, "dp", axis=2, tiled=True),
    )
    query_back, key_back, value_back, output_back, gain_one_back, gain_two_back, router_back = (
        dense_back
    )
    gate_back, up_back, down_back = expert_back
    grad_final = cotangent.astype(jnp.float32)
    grad_gates = jnp.sum(picked * grad_final[:, None, :], axis=-1)
    grad_chosen = gates * (grad_gates - jnp.sum(gates * grad_gates, axis=-1, keepdims=True))
    grad_logits = jnp.sum(grad_chosen[:, :, None] * route_hot, axis=1).astype(jnp.bfloat16)
    grad_rows = (gates[:, :, None] * grad_final[:, None, :]).astype(jnp.bfloat16).reshape(-1, width)
    grad_expert_out = (
        jnp.zeros((EXPERTS * CAP, width), jnp.bfloat16)
        .at[slot_index.reshape(-1)]
        .set(grad_rows)
        .reshape(EXPERTS, CAP, width)
    )
    grad_hidden = jnp.einsum(
        "ecd,efd->ecf", grad_expert_out, down_back, preferred_element_type=jnp.float32
    )
    silu_slope = sigmoid_gate * (1.0 + gate_act * (1.0 - sigmoid_gate))
    grad_gate_act = (grad_hidden * up_act * silu_slope).astype(jnp.bfloat16)
    grad_up_act = (grad_hidden * silu_gate).astype(jnp.bfloat16)
    grad_gathered = jnp.einsum(
        "ecf,edf->ecd", grad_gate_act, gate_back, preferred_element_type=jnp.float32
    )
    grad_gathered = (
        grad_gathered
        + jnp.einsum("ecf,edf->ecd", grad_up_act, up_back, preferred_element_type=jnp.float32)
    ).reshape(EXPERTS * CAP, width)
    grad_normed_two = jnp.sum(grad_gathered[slot_index], axis=1)
    grad_normed_two = grad_normed_two + jnp.einsum(
        "te,de->td", grad_logits, router_back, preferred_element_type=jnp.float32
    )
    router_grad = jnp.einsum(
        "td,te->de", normed_two, grad_logits, preferred_element_type=jnp.float32
    )
    down_grad = jnp.einsum(
        "ecf,ecd->efd", hidden, grad_expert_out, preferred_element_type=jnp.float32
    )
    gate_grad = jnp.einsum(
        "ecd,ecf->edf", gathered, grad_gate_act, preferred_element_type=jnp.float32
    )
    up_grad = jnp.einsum("ecd,ecf->edf", gathered, grad_up_act, preferred_element_type=jnp.float32)
    expert_grads = (
        lax.psum_scatter(gate_grad, "dp", scatter_dimension=1, tiled=True),
        lax.psum_scatter(up_grad, "dp", scatter_dimension=1, tiled=True),
        lax.psum_scatter(down_grad, "dp", scatter_dimension=2, tiled=True),
    )
    grad_resid_norm, second_gain_grad = norm_back(
        resid, second_scale, gain_two_back.astype(jnp.float32), grad_normed_two
    )
    grad_resid = grad_final + grad_resid_norm
    grad_branch = grad_resid.astype(jnp.bfloat16)
    output_weight_grad = jnp.einsum(
        "ti,td->id", attn_low, grad_branch, preferred_element_type=jnp.float32
    )
    attention_gradient = jnp.einsum(
        "td,id->ti", grad_branch, output_back, preferred_element_type=jnp.float32
    ).astype(jnp.bfloat16)
    attention_gradient = attention_gradient.reshape(
        sequence_count, sequence_length, KEY_VALUE_HEADS, query_group_width, HEAD_SIZE
    )
    query_rot_grad, key_rotated_gradient, value_rotated_gradient = lax.map(
        sequence_backward,
        (query_sequences, key_sequences, value_sequences, segments, log_totals, attention_gradient),
    )
    grad_query = (
        inverse_rotation(
            query_rot_grad.reshape(number_of_rows, QUERY_HEADS, HEAD_SIZE),
            cosine_lookup,
            sine_lookup,
        )
        .reshape(number_of_rows, QUERY_HEADS * HEAD_SIZE)
        .astype(jnp.bfloat16)
    )
    grad_key = (
        inverse_rotation(
            key_rotated_gradient.reshape(number_of_rows, KEY_VALUE_HEADS, HEAD_SIZE),
            cosine_lookup,
            sine_lookup,
        )
        .reshape(number_of_rows, KEY_VALUE_HEADS * HEAD_SIZE)
        .astype(jnp.bfloat16)
    )
    value_gradient_rows = value_rotated_gradient.reshape(
        number_of_rows, KEY_VALUE_HEADS * HEAD_SIZE
    ).astype(jnp.bfloat16)
    query_grad = jnp.einsum(
        "td,ti->di", first_normed_input, grad_query, preferred_element_type=jnp.float32
    )
    key_grad = jnp.einsum(
        "td,ti->di", first_normed_input, grad_key, preferred_element_type=jnp.float32
    )
    value_grad = jnp.einsum(
        "td,ti->di", first_normed_input, value_gradient_rows, preferred_element_type=jnp.float32
    )
    grad_normed_one = jnp.einsum(
        "ti,di->td", grad_query, query_back, preferred_element_type=jnp.float32
    )
    grad_normed_one = grad_normed_one + jnp.einsum(
        "ti,di->td", grad_key, key_back, preferred_element_type=jnp.float32
    )
    grad_normed_one = grad_normed_one + jnp.einsum(
        "ti,di->td", value_gradient_rows, value_back, preferred_element_type=jnp.float32
    )
    grad_input_norm, first_gain_grad = norm_back(
        inputs, first_scale, gain_one_back.astype(jnp.float32), grad_normed_one
    )
    input_grad = grad_resid + grad_input_norm
    dense_grads = (
        lax.psum_scatter(query_grad, "dp", scatter_dimension=0, tiled=True),
        lax.psum_scatter(key_grad, "dp", scatter_dimension=0, tiled=True),
        lax.psum_scatter(value_grad, "dp", scatter_dimension=0, tiled=True),
        lax.psum_scatter(output_weight_grad, "dp", scatter_dimension=1, tiled=True),
        lax.psum_scatter(first_gain_grad, "dp", scatter_dimension=0, tiled=True),
        lax.psum_scatter(second_gain_grad, "dp", scatter_dimension=0, tiled=True),
        lax.psum_scatter(router_grad, "dp", scatter_dimension=0, tiled=True),
    )
    return (
        output,
        input_grad,
        dense_grads[0],
        dense_grads[1],
        dense_grads[2],
        dense_grads[3],
        dense_grads[4],
        dense_grads[5],
        dense_grads[6],
        expert_grads[0],
        expert_grads[1],
        expert_grads[2],
    )


def solution(mesh):
    in_specs = (
        P("dp", None),
        P("dp", None),
        P("dp", None),
        P("dp", None),
        P(None, "dp"),
        P("dp"),
        P("dp"),
        P("dp", None),
        P(None, "dp", None),
        P(None, "dp", None),
        P(None, None, "dp"),
        P("dp", None),
        P("dp", None),
        P("dp", None),
    )
    out_specs = (
        P("dp", None),
        P("dp", None),
        P("dp", None),
        P("dp", None),
        P("dp", None),
        P(None, "dp"),
        P("dp"),
        P("dp"),
        P("dp", None),
        P(None, "dp", None),
        P(None, "dp", None),
        P(None, None, "dp"),
    )
    return jax.shard_map(local, mesh=mesh, in_specs=in_specs, out_specs=out_specs, check_vma=False)
```

profile of v0, /device:TPU:0, one launch (start us, length us, event | category | flops | bytes accessed | tf_op | source)
XLA Modules:
  0.0 2516.8 jit_solution(16343722312286233349)
XLA Ops:
  14.8 42.0 %all-reduce.5 = (bf16[1024]{0:T(1024)(128)(2,1)S(1)}, bf16[1024]{0:T(1024)(128)(2,1)S(1)}) all-reduce(bf16[1024]{0:T(1024)(128)(2,1)S(1)} %dynamic-update-slice.4, bf16[1024]{0:T(1024)(128)(2,1)S(1)} %dynamic-update-slice.5), channel_id=1, replica_groups=mesh['dp'=32] {'dp'}, use_global_device_ids=true, to_apply=%add | all-reduce | flops 2048 | bytes 8192
  56.8 40.8 %all-gather = bf16[32,32,16]{1,2,0:T(8,128)(2,1)S(1)} all-gather(bf16[1,32,16]{1,2,0:T(8,128)(2,1)} %bitcast.180), channel_id=1, replica_groups=mesh['dp'=32] {'dp'}, dimensions={0}, use_global_device_ids=true | all-gather | bytes 33792 | tf_op jit(solution)/shard_map/all_gather | solution.py:196
  98.5 4.6 reduce-window.6
  104.7 15.5 scatter_custom_fusion.1
  120.3 15.5 scatter_custom_fusion
  146.8 34.5 %all-gather.13.cloned.1.call-done = bf16[1024,1024]{1,0:T(8,128)(2,1)} async-done(((bf16[32,1024]{1,0:T(8,128)(2,1)}), bf16[1024,1024]{1,0:T(8,128)(2,1)}) %all-gather.13.cloned.1.call-update) | async-done | bytes 2097168 | tf_op jit(solution)/shard_map/all_gather | solution.py:190
  184.8 18.6 fusion.83
  203.4 8.3 fusion.6
  211.7 8.5 fusion.35
  220.2 19.0 all-gather.15.cloned.1.call-done
  239.3 3.3 multiply_reduce_fusion.2
  245.8 14.9 gather_fusion
  260.8 25.9 %scatter_custom_fusion.2 = bf16[4608,1024]{1,0:T(8,128)(2,1)} fusion(s32[4096]{0:T(1024)} %bitcast.178, f32[512,1024]{1,0:T(8,128)S(1)} %convert_element_type.108, f32[4096]{0:T(1024)S(1)} %div.101, bf16[]{:T(256)} %constant.181.clone.1), kind=kCustom, calls=%fused_computation.31 | custom fusion | flops 8388608 | bytes 11551232 | tf_op jit(solution)/shard_map/scatter | solution.py:283
  287.3 68.6 %all-gather.19.cloned.1.call-done = bf16[16,1024,512]{2,1,0:T(8,128)(2,1)} async-done(((bf16[16,32,512]{2,1,0:T(8,128)(2,1)}), bf16[16,1024,512]{2,1,0:T(8,128)(2,1)}) %all-gather.19.cloned.1.call-update) | async-done | bytes 16777232 | tf_op jit(solution)/shard_map/all_gather | solution.py:200
  355.9 15.2 fusion.19
  371.2 100.8 %all-gather.17.cloned.1.call-done = bf16[16,1024,512]{2,1,0:T(8,128)(2,1)} async-done(((bf16[16,32,512]{2,1,0:T(8,128)(2,1)}), bf16[16,1024,512]{2,1,0:T(8,128)(2,1)}) %all-gather.17.cloned.1.call-update) | async-done | bytes 16777232 | tf_op jit(solution)/shard_map/all_gather | solution.py:199
  472.0 14.8 fusion.20
  486.8 101.4 %all-gather.21.cloned.1.call-done = bf16[16,512,1024]{1,2,0:T(8,128)(2,1)} async-done(((bf16[16,512,32]{1,2,0:T(8,128)(2,1)}), bf16[16,512,1024]{1,2,0:T(8,128)(2,1)}) %all-gather.21.cloned.1.call-update) | async-done | bytes 16777232 | tf_op jit(solution)/shard_map/all_gather | solution.py:201
  588.2 25.0 multiply_convert_fusion
  613.3 13.4 fusion.86
  626.7 19.8 convolution_add_fusion
  646.5 28.7 %gather_fusion.2 = f32[4096,1024]{1,0:T(8,128)} fusion(f32[4608,1024]{1,0:T(8,128)} %bitcast.142, s32[4096]{0:T(1024)S(1)} %copy-done.11), kind=kCustom, calls=%fused_computation.2 | custom fusion | bytes 33570816 | tf_op jit(solution)/shard_map/gather | solution.py:299
  675.2 9.6 bitcast_reduce_fusion
  684.8 13.4 fusion.85
  698.2 28.7 %gather_fusion.1 = f32[4096,1024]{1,0:T(8,128)} fusion(f32[4608,1024]{1,0:T(8,128)} %bitcast.141, s32[4096]{0:T(1024)S(1)} %copy-done.11), kind=kCustom, calls=%fused_computation.1 | custom fusion | bytes 33570816 | tf_op jit(solution)/shard_map/gather | solution.py:255
  727.0 11.2 fusion.4
  740.8 3.7 multiply_reduce_fusion
  744.6 4.0 subtract_add_fusion
  752.0 8.9 fusion.41
  764.1 7.9 fusion
  772.1 8.3 fusion.2
  780.5 4.3 fusion.40
  788.2 4.5 fusion.45
  793.2 5.0 convolution_multiply_fusion
  799.6 3.4 fusion.76
  803.1 18.4 fusion.89
  822.2 18.6 fusion.17
  841.0 18.6 fusion.18
  861.9 3.3 fusion.87
  867.8 38.9 %all-reduce.4 = (f32[1024]{0:T(1024)S(1)}, f32[1024]{0:T(1024)S(1)}) all-reduce(f32[1024]{0:T(1024)S(1)} %get-tuple-element.117, f32[1024]{0:T(1024)S(1)} %get-tuple-element.115), channel_id=6, replica_groups=mesh['dp'=32] {'dp'}, use_global_device_ids=true, to_apply=%region_26.27.clone | all-reduce | flops 2048 | bytes 16384
  907.9 3.5 fusion.31
  912.8 100.0 %reduce-scatter.15.cloned.1.call-done = f32[32,512]{1,0:T(8,128)} async-done(((f32[1024,512]{1,0:T(8,128)}), f32[32,512]{1,0:T(8,128)}) %reduce-scatter.15.cloned.1.call-update) | async-done | bytes 65552 | tf_op jit(solution)/shard_map/reduce_scatter | solution.py:382
  1012.8 135.2 %reduce-scatter.13.cloned.1.call-done = f32[32,512]{1,0:T(8,128)} async-done(((f32[1024,512]{1,0:T(8,128)}), f32[32,512]{1,0:T(8,128)}) %reduce-scatter.13.cloned.1.call-update) | async-done | bytes 65552 | tf_op jit(solution)/shard_map/reduce_scatter | solution.py:381
  1148.0 139.8 %reduce-scatter.17.cloned.1.call-done = f32[1024,32]{0,1:T(8,128)} async-done(((f32[1024,1024]{0,1:T(8,128)}), f32[1024,32]{0,1:T(8,128)}) %reduce-scatter.17.cloned.1.call-update) | async-done | bytes 131088 | tf_op jit(solution)/shard_map/reduce_scatter | solution.py:383
  1287.8 139.4 %reduce-scatter.11.cloned.1.call-done = f32[32,1024]{1,0:T(8,128)} async-done(((f32[1024,1024]{1,0:T(8,128)}), f32[32,1024]{1,0:T(8,128)}) %reduce-scatter.11.cloned.1.call-update) | async-done | bytes 131088 | tf_op jit(solution)/shard_map/reduce_scatter | solution.py:380
  1427.2 353.3 %reduce-scatter.23.cloned.1.call-done = f32[16,512,32]{1,2,0:T(8,128)} async-done(((f32[16,512,1024]{1,2,0:T(8,128)}), f32[16,512,32]{1,2,0:T(8,128)}) %reduce-scatter.23.cloned.1.call-update) | async-done | bytes 1048592 | tf_op jit(solution)/shard_map/reduce_scatter | solution.py:316
  1780.5 364.8 %reduce-scatter.21.cloned.1.call-done = f32[16,32,512]{2,1,0:T(8,128)} async-done(((f32[16,1024,512]{2,1,0:T(8,128)}), f32[16,32,512]{2,1,0:T(8,128)}) %reduce-scatter.21.cloned.1.call-update) | async-done | bytes 1048592 | tf_op jit(solution)/shard_map/reduce_scatter | solution.py:315
  2145.3 364.8 %reduce-scatter.19.cloned.1.call-done = f32[16,32,512]{2,1,0:T(8,128)} async-done(((f32[16,1024,512]{2,1,0:T(8,128)}), f32[16,32,512]{2,1,0:T(8,128)}) %reduce-scatter.19.cloned.1.call-update) | async-done | bytes 1048592 | tf_op jit(solution)/shard_map/reduce_scatter | solution.py:314
  (230 shorter events, 50.5 us)
Async XLA Ops:
  7.2 133.7 %all-gather.11.cloned.1.call-start = ((), (), s32[]{:S(2)}) async-start(), calls=%async_computation.9 | async-start | bytes 1081344 | tf_op jit(solution)/shard_map/all_gather | solution.py:191
  7.9 135.9 %all-gather.9.cloned.1.call-start = ((), (), s32[]{:S(2)}) async-start(), calls=%async_computation.8 | async-start | bytes 1081344 | tf_op jit(solution)/shard_map/all_gather | solution.py:192
  8.7 172.6 %all-gather.13.cloned.1.call-start = ((), (), s32[]{:S(2)}) async-start(), calls=%async_computation.10 | async-start | bytes 2162688 | tf_op jit(solution)/shard_map/all_gather | solution.py:190
  9.4 229.9 %all-gather.15.cloned.1.call-start = ((), (), s32[]{:S(2)}) async-start(), calls=%async_computation.11 | async-start | bytes 2162688 | tf_op jit(solution)/shard_map/all_gather | solution.py:193
  10.0 346.0 %all-gather.19.cloned.1.call-start = ((), (), s32[]{:S(2)}) async-start(), calls=%async_computation.13 | async-start | bytes 17301504 | tf_op jit(solution)/shard_map/all_gather | solution.py:200
  10.6 127.6 %copy-start.3 = (bf16[512,1024]{1,0:T(8,128)(2,1)S(1)}, bf16[512,1024]{1,0:T(8,128)(2,1)}, u32[]{:S(2)}) copy-start(bf16[512,1024]{1,0:T(8,128)(2,1)} %param.22) | copy-start | bytes 3145732
  10.6 461.4 %all-gather.17.cloned.1.call-start = ((), (), s32[]{:S(2)}) async-start(), calls=%async_computation.12 | async-start | bytes 17301504 | tf_op jit(solution)/shard_map/all_gather | solution.py:199
  11.1 577.1 %all-gather.21.cloned.1.call-start = ((), (), s32[]{:S(2)}) async-start(), calls=%async_computation.14 | async-start | bytes 17301504 | tf_op jit(solution)/shard_map/all_gather | solution.py:201
  11.9 899.5 %reduce-scatter.25.cloned.1.call-start = ((), (), s32[]{:S(2)}) async-start(), calls=%async_computation.22 | async-start | bytes 540672
  13.0 127.0 %copy-start.60 = (s32[1,512]{1,0:T(1,128)S(1)}, s32[1,512]{1,0:T(1,128)}, u32[]{:S(2)}) copy-start(s32[1,512]{1,0:T(1,128)} %param.34) | copy-start | bytes 6148
  56.8 124.5 %copy-start.46 = (f32[1024]{0:T(1024)}, f32[1024]{0:T(1024)S(1)}, u32[]{:S(2)}) copy-start(f32[1024]{0:T(1024)S(1)} %convert_element_type.96) | copy-start | bytes 12292
  56.8 186.4 %copy-start.49 = (f32[1024]{0:T(1024)}, f32[1024]{0:T(1024)S(1)}, u32[]{:S(2)}) copy-start(f32[1024]{0:T(1024)S(1)} %convert_element_type.103) | copy-start | bytes 12292
  104.7 15.6 copy-start.59
  135.9 336.1 %copy-start.37 = (pred[16,288]{1,0:T(8,128)(4,1)}, pred[16,288]{1,0:T(8,128)(4,1)S(1)}, u32[]{:S(2)}) copy-start(pred[16,288]{1,0:T(8,128)(4,1)S(1)} %broadcast_in_dim.66) | copy-start | bytes 13828
  137.4 123.4 %copy-start.10 = (f32[512,1024]{1,0:T(8,128)}, f32[512,1024]{1,0:T(8,128)S(1)}, u32[]{:S(2)}) copy-start(f32[512,1024]{1,0:T(8,128)S(1)} %convert_element_type.108) | copy-start | bytes 6291460
  140.0 44.4 %copy-start.22 = (f32[512,32]{0,1:T(8,128)}, f32[512,32]{0,1:T(8,128)S(1)}, u32[]{:S(2)}) copy-start(f32[512,32]{0,1:T(8,128)S(1)} %get-tuple-element.142) | copy-start | bytes 196612
  140.0 44.4 %copy-start.24 = (f32[512,32]{0,1:T(8,128)}, f32[512,32]{0,1:T(8,128)S(1)}, u32[]{:S(2)}) copy-start(f32[512,32]{0,1:T(8,128)S(1)} %get-tuple-element.143) | copy-start | bytes 196612
  143.8 40.9 %copy-start.29 = (bf16[512,8,32]{0,2,1:T(8,128)(2,1)}, bf16[512,8,32]{0,2,1:T(8,128)(2,1)S(1)}, u32[]{:S(2)}) copy-start(bf16[512,8,32]{0,2,1:T(8,128)(2,1)S(1)} %get-tuple-element.134) | copy-start | bytes 786436
  184.7 18.6 copy-start.19
  184.7 18.6 copy-start.21
  243.3 17.5 copy-start.57
  244.2 16.6 copy-start
  245.4 15.4 copy-start.17
  260.8 25.9 %copy-start.45 = (f32[8,2,512]{2,1,0:T(2,128)S(1)}, f32[8,2,512]{2,1,0:T(2,128)}, u32[]{:S(2)}) copy-start(f32[8,2,512]{2,1,0:T(2,128)} %copy-done.44) | copy-start | bytes 98308
  626.7 19.8 copy-start.11
  698.2 28.7 %copy-start.18 = (f32[512,8]{1,0:T(8,128)S(1)}, f32[512,8]{1,0:T(8,128)}, u32[]{:S(2)}) copy-start(f32[512,8]{1,0:T(8,128)} %copy-done.17) | copy-start | bytes 49156
  726.9 12.4 copy-start.33
  726.9 12.4 copy-start.54
  726.9 12.4 copy-start.56
  726.9 12.4 copy-start.43
  726.9 12.5 copy-start.1
  727.0 13.8 copy-start.9
  727.0 13.8 copy-start.40
  727.0 13.8 copy-start.50
  727.0 13.8 copy-start.58
  744.5 268.2 %reduce-scatter.15.cloned.1.call-start = ((), (), s32[]{:S(2)}) async-start(), calls=%async_computation.17 | async-start | bytes 2162688 | tf_op jit(solution)/shard_map/reduce_scatter | solution.py:382
  752.0 8.9 copy-start.12
  752.0 9.7 copy-start.4
  752.0 9.7 copy-start.47
  752.0 9.7 copy-start.52
  764.0 383.9 %reduce-scatter.13.cloned.1.call-start = ((), (), s32[]{:S(2)}) async-start(), calls=%async_computation.16 | async-start | bytes 2162688 | tf_op jit(solution)/shard_map/reduce_scatter | solution.py:381
  772.1 8.4 copy-start.20
  788.1 499.7 %reduce-scatter.17.cloned.1.call-start = ((), (), s32[]{:S(2)}) async-start(), calls=%async_computation.18 | async-start | bytes 4325376 | tf_op jit(solution)/shard_map/reduce_scatter | solution.py:383
  792.7 634.5 %reduce-scatter.11.cloned.1.call-start = ((), (), s32[]{:S(2)}) async-start(), calls=%async_computation.15 | async-start | bytes 4325376 | tf_op jit(solution)/shard_map/reduce_scatter | solution.py:380
  803.1 977.4 %reduce-scatter.23.cloned.1.call-start = ((), (), s32[]{:S(2)}) async-start(), calls=%async_computation.21 | async-start | bytes 34603008 | tf_op jit(solution)/shard_map/reduce_scatter | solution.py:316
  821.6 1323.7 %reduce-scatter.21.cloned.1.call-start = ((), (), s32[]{:S(2)}) async-start(), calls=%async_computation.20 | async-start | bytes 34603008 | tf_op jit(solution)/shard_map/reduce_scatter | solution.py:315
  840.8 1669.2 %reduce-scatter.19.cloned.1.call-start = ((), (), s32[]{:S(2)}) async-start(), calls=%async_computation.19 | async-start | bytes 34603008 | tf_op jit(solution)/shard_map/reduce_scatter | solution.py:314
  865.2 42.7 %copy-start.61 = (f32[512]{0:T(512)S(1)}, f32[512]{0:T(512)}, u32[]{:S(2)}) copy-start(f32[512]{0:T(512)} %get-tuple-element.138) | copy-start | bytes 6148
  (31 other events, 108.9 us)
Sparse Core Ops, SparseCore 0:
  10.9 56.4 all-gather.10
  70.2 52.7 all-gather.8
  125.9 55.3 all-gather.12
  184.0 55.2 all-gather.14
  242.1 113.8 all-gather.18
  358.7 113.2 all-gather.16
  474.9 113.2 all-gather.20
  744.7 132.3 reduce-scatter.24
  879.9 132.7 reduce-scatter.14
  1015.4 132.4 reduce-scatter.12
  1150.9 136.7 reduce-scatter.16
  1290.6 136.5 reduce-scatter.10
  1430.2 350.2 reduce-scatter.22
  1783.3 361.9 reduce-scatter.20
  2148.1 361.9 reduce-scatter.18
where the time goes:
time: 2530 us; the launch traced here: 2520 us
  waiting for transfers between devices  1930 us (76%)
  matrix products  249 us (10%)
  blocking collectives  122 us (5%)
  local copies, waits for them, and re-layouts  119 us (5%)
  other arithmetic  84.4 us (3%)
    reduce_scatter x1, waiting for transfers between devices, local(): lax.psum_scatter(up_grad, 'dp', scatter_dimension=1, tiled=True)  365 us
    reduce_scatter x1, waiting for transfers between devices, local(): lax.psum_scatter(gate_grad, 'dp', scatter_dimension=1, tiled=True)  365 us
    reduce_scatter x1, waiting for transfers between devices, local(): lax.psum_scatter(down_grad, 'dp', scatter_dimension=2, tiled=True)  353 us
    reduce_scatter x1, waiting for transfers between devices, local(): lax.psum_scatter(output_weight_grad, 'dp', scatter_dimension=1, tiled=True)  140 us
    reduce_scatter x1, waiting for transfers between devices, local(): lax.psum_scatter(query_grad, 'dp', scatter_dimension=0, tiled=True)  139 us
    reduce_scatter x1, waiting for transfers between devices, local(): lax.psum_scatter(key_grad, 'dp', scatter_dimension=0, tiled=True)  135 us
    all_gather x1, waiting for transfers between devices, local(): lax.all_gather(down_weight, 'dp', axis=2, tiled=True)  101 us
    all_gather x1, waiting for transfers between devices, local(): lax.all_gather(gate_weight, 'dp', axis=1, tiled=True)  101 us
  transfers between devices with their start and end apart: 15, of which 12 were waited for; matrix products, arithmetic and copies ran while one was open for 12% of the time, Pallas kernels for 0%

commit v1 on v0

v1 whole, which is shorter than its diff:
```python
import math

import jax
import jax.numpy as jnp
from jax import lax
from jax.sharding import PartitionSpec as P

QUERY_HEADS = 16
KEY_VALUE_HEADS = 8
HEAD_SIZE = 64
EXPERTS = 16
PLANE = 8
MINE = EXPERTS // PLANE

epsilon = 1e-06
neg_large = -1000000000.0
BF = jnp.bfloat16
F32 = jnp.float32


def dot(a, b, ca, cb):
    return lax.dot_general(a, b, (((ca,), (cb,)), ((), ())), preferred_element_type=F32)


def rms_scale(values):
    return lax.rsqrt(jnp.mean(values * values, axis=-1, keepdims=True) + epsilon)


def norm_back(values, scale_rows, gain_full, grad_out):
    weighted = grad_out * gain_full
    gain_grad = jnp.sum(grad_out * values * scale_rows, axis=0)
    inner_mean = jnp.mean(weighted * values, axis=-1, keepdims=True)
    grad_in = scale_rows * weighted - values * (scale_rows * scale_rows * scale_rows) * inner_mean
    return (grad_in, gain_grad)


def rope_tables(sequence_length, head_dim, copies):
    positions = jnp.arange(sequence_length, dtype=jnp.float32)
    frequency = 10000.0 ** (-2.0 * jnp.arange(head_dim // 2, dtype=jnp.float32) / head_dim)
    angles = jnp.tile(positions[:, None] * frequency[None, :], (copies, 1))
    return (jnp.cos(angles), jnp.sin(angles))


def rotate(values, cosine_lookup, sine_lookup):
    half_dim = values.shape[-1] // 2
    first_half = values[..., :half_dim]
    second_half = values[..., half_dim:]
    cos_part = cosine_lookup[:, None, :]
    sin_part = sine_lookup[:, None, :]
    return jnp.concatenate(
        [
            first_half * cos_part - second_half * sin_part,
            second_half * cos_part + first_half * sin_part,
        ],
        axis=-1,
    )


def attention_forward(query, key, value, allowed, score_scale):
    raw_scores = jnp.einsum("qgrd,kgd->grqk", query, key, preferred_element_type=F32)
    scores = jnp.where(allowed, raw_scores * score_scale, neg_large)
    largest = jnp.max(scores, axis=-1, keepdims=True)
    exponent = jnp.exp(scores - largest)
    totals = jnp.sum(exponent, axis=-1, keepdims=True)
    prob_low = (exponent / totals).astype(BF)
    mixed = jnp.einsum("grqk,kgd->qgrd", prob_low, value, preferred_element_type=F32)
    return mixed, largest + jnp.log(totals)


def attention_backward(query, key, value, allowed, log_total, grad, score_scale):
    raw_scores = jnp.einsum("qgrd,kgd->grqk", query, key, preferred_element_type=F32)
    scores = jnp.where(allowed, raw_scores * score_scale, neg_large)
    prob = jnp.exp(scores - log_total)
    grad_probs = jnp.einsum("qgrd,kgd->grqk", grad, value, preferred_element_type=F32)
    inner = jnp.sum(prob * grad_probs, axis=-1, keepdims=True)
    grad_scores = (prob * (grad_probs - inner)).astype(BF)
    grad_query = jnp.einsum("grqk,kgd->qgrd", grad_scores, key, preferred_element_type=F32)
    grad_key = jnp.einsum("grqk,qgrd->kgd", grad_scores, query, preferred_element_type=F32)
    grad_value = jnp.einsum("grqk,qgrd->kgd", prob.astype(BF), grad, preferred_element_type=F32)
    return grad_query * score_scale, grad_key * score_scale, grad_value


def make_local(n):
    plane_groups = [[PLANE * z + i for i in range(PLANE)] for z in range(n // PLANE)]
    outer_groups = [[PLANE * z + i for z in range(n // PLANE)] for i in range(PLANE)]

    def swap(array, offset):
        return lax.ppermute(array, "dp", [(i, i ^ offset) for i in range(n)])

    def plane_gather(block):
        half = block.shape[0] // 2
        by_x, by_y = swap(block, 2), swap(block, 4)
        corner = jnp.concatenate([swap(by_y[:half], 2), swap(by_x[half:], 4)], axis=0)
        same_core = [block, by_x, by_y, corner]
        other_core = [swap(part, 1) for part in same_core]
        return [part for pair in zip(same_core, other_core) for part in pair]

    def plane_sum(parts):
        def up(v):
            return v.astype(F32)

        s0, s2, s4, s6 = (up(parts[k]) + up(swap(parts[k + 1], 1)) for k in (0, 2, 4, 6))
        half = s6.shape[0] // 2
        s6 = s6.astype(BF)
        s4 = jnp.concatenate([s4[:half] + up(swap(s6[:half], 2)), s4[half:]], axis=0)
        s2 = jnp.concatenate([s2[:half], s2[half:] + up(swap(s6[half:], 4))], axis=0)
        return s0 + up(swap(s2.astype(BF), 2)) + up(swap(s4.astype(BF), 4))

    def local(
        tokens,
        query_weight,
        key_projection_weight,
        value_projection_weight,
        output_weight,
        first_gain,
        second_gain,
        router_weight,
        gate_weight,
        up_weight,
        down_weight,
        routes,
        segments,
        cotangent,
    ):
        rows, width = tokens.shape
        ff = gate_weight.shape[2]
        share = query_weight.shape[0]
        me = lax.axis_index("dp")
        place = lax.rem(me, PLANE)

        dense_part = jnp.concatenate(
            [
                query_weight,
                key_projection_weight,
                value_projection_weight,
                output_weight.T,
                router_weight,
                first_gain[:, None],
                second_gain[:, None],
                jnp.zeros((share, 128 - EXPERTS - 2), BF),
            ],
            axis=1,
        )
        dense = lax.all_gather(dense_part, "dp", axis=0, tiled=True)
        query_full, key_full, value_full = dense[:, :1024], dense[:, 1024:1536], dense[:, 1536:2048]
        output_turned = dense[:, 2048:3072]
        router_full = dense[:, 3072 : 3072 + EXPERTS]
        gain_one = dense[:, 3072 + EXPERTS].astype(F32)
        gain_two = dense[:, 3073 + EXPERTS].astype(F32)

        def by_owner(w):
            return w.transpose(1, 0, 2).reshape(share, PLANE, MINE * ff)

        expert_part = jnp.concatenate(
            [by_owner(gate_weight), by_owner(up_weight), by_owner(down_weight.transpose(0, 2, 1))],
            axis=2,
        ).transpose(1, 0, 2)
        expert_part = lax.all_to_all(
            expert_part, "dp", split_axis=0, concat_axis=0, axis_index_groups=plane_groups
        ).reshape(PLANE * share, 3 * MINE * ff)
        expert_full = lax.all_gather(
            expert_part, "dp", axis=0, tiled=True, axis_index_groups=outer_groups
        )
        wide = MINE * ff
        gate_full, up_full, down_turned = (expert_full[:, k * wide : (k + 1) * wide] for k in range(3))

        route_mask = jnp.sum(
            routes[:, :, None] == jnp.arange(EXPERTS, dtype=jnp.int32)[None, None, :], axis=1
        ).astype(F32)
        grads_plane = jnp.concatenate(plane_gather(cotangent), axis=0)

        cosine, sine = rope_tables(rows, HEAD_SIZE, 1)
        inputs = tokens.astype(F32)
        first_scale = rms_scale(inputs)
        normed_one = (inputs * first_scale * gain_one).astype(BF)
        query = dot(normed_one, query_full, 1, 0).reshape(rows, QUERY_HEADS, HEAD_SIZE)
        key = dot(normed_one, key_full, 1, 0).reshape(rows, KEY_VALUE_HEADS, HEAD_SIZE)
        value = dot(normed_one, value_full, 1, 0).astype(BF).reshape(rows, KEY_VALUE_HEADS, HEAD_SIZE)
        query = rotate(query, cosine, sine).astype(BF)
        key = rotate(key, cosine, sine).astype(BF)
        query = query.reshape(rows, KEY_VALUE_HEADS, QUERY_HEADS // KEY_VALUE_HEADS, HEAD_SIZE)
        seg = segments[0]
        positions = jnp.arange(rows, dtype=jnp.int32)
        allowed = (seg[:, None] == seg[None, :]) & (positions[:, None] >= positions[None, :])
        score_scale = 1.0 / math.sqrt(HEAD_SIZE)
        mixed, log_total = attention_forward(query, key, value, allowed, score_scale)
        mixed = mixed.reshape(rows, QUERY_HEADS * HEAD_SIZE).astype(BF)
        resid = inputs + dot(mixed, output_turned, 1, 1)
        second_scale = rms_scale(resid)
        normed_two = (resid * second_scale * gain_two).astype(BF)
        logits = dot(normed_two, router_full, 1, 0)
        masked = jnp.where(route_mask > 0, logits, neg_large)
        top = jnp.max(masked, axis=-1, keepdims=True)
        weight = jnp.exp(masked - top) * route_mask
        gates = weight / jnp.sum(weight, axis=-1, keepdims=True)

        gate_rows = gates.T
        gate_high = gate_rows.astype(BF)
        gate_low = (gate_rows - gate_high.astype(F32)).astype(BF)
        packed = jnp.concatenate([gate_high, gate_low], axis=1).reshape(EXPERTS, 2 * rows)
        sent = jnp.concatenate([normed_two, packed.reshape(-1, width)], axis=0)
        got = plane_gather(sent)
        tokens_plane = jnp.concatenate([b[:rows] for b in got], axis=0)

        def my_gates(b):
            halves = b[rows:].reshape(EXPERTS, 2, rows)
            own = lax.dynamic_slice_in_dim(halves, place * MINE, MINE, axis=0).astype(F32)
            return own[:, 0] + own[:, 1]

        gates_mine = jnp.concatenate([my_gates(b) for b in got], axis=1)
        gate_cols = gates_mine.T
        gate_wide = jnp.repeat(gate_cols, ff, axis=1)

        act_a = dot(tokens_plane, gate_full, 1, 0)
        act_b = dot(tokens_plane, up_full, 1, 0)
        grad_down = dot(grads_plane, down_turned, 1, 0)
        sigma = jax.nn.sigmoid(act_a)
        silu = act_a * sigma
        hidden = (silu * act_b).astype(BF).astype(F32)
        gate_grad_rows = jnp.sum((hidden * grad_down).reshape(-1, MINE, ff), axis=2)
        hidden_gated = (hidden * gate_wide).astype(BF)
        grad_hidden = grad_down * gate_wide
        grad_a = (grad_hidden * act_b * (sigma * (1.0 + act_a * (1.0 - sigma)))).astype(BF)
        grad_b = (grad_hidden * silu).astype(BF)
        grad_tokens = (dot(grad_a, gate_full, 1, 1) + dot(grad_b, up_full, 1, 1)).astype(BF)
        expert_out = dot(hidden_gated, down_turned, 1, 1).astype(BF)
        gate_grad = dot(tokens_plane, grad_a, 0, 0)
        up_grad = dot(tokens_plane, grad_b, 0, 0)
        down_grad = dot(grads_plane, hidden_gated, 0, 0)

        back_rows = gate_grad_rows.reshape(PLANE, rows, MINE).transpose(0, 2, 1)
        back_high = back_rows.astype(BF)
        back_low = (back_rows - back_high.astype(F32)).astype(BF)
        back = jnp.concatenate([back_high, back_low], axis=2)
        back = lax.dynamic_update_slice_in_dim(
            jnp.zeros((PLANE, EXPERTS, 2 * rows), BF), back, place * MINE, axis=1
        ).reshape(PLANE, -1, width)
        blocks = [
            jnp.concatenate([grad_tokens[k * rows : (k + 1) * rows], back[k]], axis=0)
            for k in range(PLANE)
        ]
        returned = plane_sum(blocks)
        grad_normed_two = returned[:rows]
        halves = returned[rows:].reshape(EXPERTS, 2, rows)
        grad_gates = (halves[:, 0] + halves[:, 1]).T
        experts_sum = plane_sum([expert_out[k * rows : (k + 1) * rows] for k in range(PLANE)])
        output = (resid + experts_sum).astype(BF)

        expert_grads = jnp.concatenate([gate_grad, up_grad, down_grad], axis=1).astype(BF)
        expert_grads = lax.psum_scatter(
            expert_grads, "dp", scatter_dimension=0, tiled=True, axis_index_groups=outer_groups
        )
        expert_grads = lax.all_to_all(
            expert_grads.reshape(PLANE, share, 3 * wide),
            "dp",
            split_axis=0,
            concat_axis=0,
            axis_index_groups=plane_groups,
        )
        expert_grads = expert_grads.reshape(PLANE, share, 3, MINE, ff).astype(F32)
        gate_out, up_out, down_out = (
            expert_grads[:, :, k].transpose(0, 2, 1, 3).reshape(EXPERTS, share, ff) for k in range(3)
        )
        down_out = down_out.transpose(0, 2, 1)

        grad_final = cotangent.astype(F32)
        grad_chosen = gates * (grad_gates - jnp.sum(gates * grad_gates, axis=-1, keepdims=True))
        grad_logits = grad_chosen.astype(BF)
        grad_normed_two = grad_normed_two + dot(grad_logits, router_full, 1, 1)
        router_grad = dot(normed_two, grad_logits, 0, 0)
        grad_resid_norm, second_gain_grad = norm_back(resid, second_scale, gain_two, grad_normed_two)
        grad_resid = grad_final + grad_resid_norm
        grad_branch = grad_resid.astype(BF)
        output_turned_grad = dot(grad_branch, mixed, 0, 0)
        attention_gradient = dot(grad_branch, output_turned, 1, 0).astype(BF).reshape(query.shape)
        grad_query, grad_key, grad_value = attention_backward(
            query, key, value, allowed, log_total, attention_gradient, score_scale
        )
        grad_query = rotate(grad_query.reshape(rows, QUERY_HEADS, HEAD_SIZE), cosine, -sine)
        grad_key = rotate(grad_key.reshape(rows, KEY_VALUE_HEADS, HEAD_SIZE), cosine, -sine)
        grad_qkv = jnp.concatenate(
            [grad_query.reshape(rows, -1), grad_key.reshape(rows, -1), grad_value.reshape(rows, -1)],
            axis=1,
        ).astype(BF)
        qkv_grad = dot(normed_one, grad_qkv, 0, 0)
        grad_normed_one = dot(grad_qkv, dense[:, :2048], 1, 1)
        grad_input_norm, first_gain_grad = norm_back(inputs, first_scale, gain_one, grad_normed_one)
        input_grad = grad_resid + grad_input_norm

        dense_grads = jnp.concatenate(
            [
                qkv_grad,
                output_turned_grad,
                router_grad,
                first_gain_grad[:, None],
                second_gain_grad[:, None],
                jnp.zeros((width, 128 - EXPERTS - 2), F32),
            ],
            axis=1,
        ).astype(BF)
        dense_grads = lax.psum_scatter(dense_grads, "dp", scatter_dimension=0, tiled=True).astype(F32)
        return (
            output,
            input_grad,
            dense_grads[:, :1024],
            dense_grads[:, 1024:1536],
            dense_grads[:, 1536:2048],
            dense_grads[:, 2048:3072].T,
            dense_grads[:, 3072 + EXPERTS],
            dense_grads[:, 3073 + EXPERTS],
            dense_grads[:, 3072 : 3072 + EXPERTS],
            gate_out,
            up_out,
            down_out,
        )

    return local


def solution(mesh):
    in_specs = (
        P("dp", None),
        P("dp", None),
        P("dp", None),
        P("dp", None),
        P(None, "dp"),
        P("dp"),
        P("dp"),
        P("dp", None),
        P(None, "dp", None),
        P(None, "dp", None),
        P(None, None, "dp"),
        P("dp", None),
        P("dp", None),
        P("dp", None),
    )
    out_specs = (
        P("dp", None),
        P("dp", None),
        P("dp", None),
        P("dp", None),
        P("dp", None),
        P(None, "dp"),
        P("dp"),
        P("dp"),
        P("dp", None),
        P(None, "dp", None),
        P(None, "dp", None),
        P(None, None, "dp"),
    )
    return jax.shard_map(
        make_local(mesh.shape["dp"]), mesh=mesh, in_specs=in_specs, out_specs=out_specs, check_vma=False
    )
```

time: 2530 us -> 748 us (0.30)
  waiting for transfers between devices: 1930 us -> 277 us
  blocking collectives: 122 us -> 0 us
  starting transfers between devices: 1.17 us -> 39.8 us
  matrix products: 249 us -> 222 us
    reduce_scatter x7 -> x2, waiting for transfers between devices: 1600 us -> 90.2 us  [the longest x1 90.2 us: local(): lax.psum_scatter(dense_grads, 'dp', scatter_dimension=0, tiled=True)]
    all_gather x7 -> x2, waiting for transfers between devices: 324 us -> 31.5 us  [the longest x1 17.1 us: local(): lax.all_gather(expert_part, 'dp', axis=0, tiled=True, axis_index_groups=o...]
    ppermute x0 -> x32, waiting for transfers between devices: none -> 114 us  [swap(): return lax.ppermute(array, 'dp', [(i, i ^ offset) for i in range(n)])]
    unnamed x2 -> x0, blocking collectives: 80.9 us -> none
    gather x3 -> x0, local copies, waits for them, and re-layouts: 72.3 us -> none  [the longest x1 28.7 us: local(): picked = expert_out[slot_index]]
    all_to_all x0 -> x2, waiting for transfers between devices: none -> 41.1 us  [the longest x1 32.9 us: local(): lax.all_to_all(expert_grads.reshape(PLANE, share, 3 * wide), 'dp', split_...]
    all_gather x1 -> x0, blocking collectives: 40.8 us -> none  [local(): lax.all_gather(router_weight, 'dp', axis=0, tiled=True)]
    ppermute x0 -> x32, starting transfers between devices: none -> 31.3 us  [swap(): return lax.ppermute(array, 'dp', [(i, i ^ offset) for i in range(n)])]
  transfers between devices with their start and end apart: 15 -> 38, of which waited for: 12 -> 14; matrix products, arithmetic and copies ran while one was open for 12% -> 34% of each run, Pallas kernels for 0% -> 0%
where the time goes in v1:
time: 748 us; the launch traced here: 740 us
  waiting for transfers between devices  277 us (37%)
  matrix products  222 us (30%)
  local copies, waits for them, and re-layouts  94.8 us (13%)
  other arithmetic  90.1 us (12%)
  starting transfers between devices  39.8 us (5%)
  between operations  15.6 us (2%)
    dot_general x20, matrix products, dot(): lax.dot_general(a, b, (((ca,), (cb,)), ((), ())), preferred_element_type=...  179 us
    ppermute x32, waiting for transfers between devices, swap(): return lax.ppermute(array, 'dp', [(i, i ^ offset) for i in range(n)])  114 us
    reduce_scatter x1, waiting for transfers between devices, local(): lax.psum_scatter(dense_grads, 'dp', scatter_dimension=0, tiled=True)  90.2 us
    unnamed x143, local copies, waits for them, and re-layouts  37.3 us
    all_to_all x1, waiting for transfers between devices, local(): lax.all_to_all(expert_grads.reshape(PLANE, share, 3 * wide), 'dp', split_...  32.9 us
    ppermute x32, starting transfers between devices, swap(): return lax.ppermute(array, 'dp', [(i, i ^ offset) for i in range(n)])  31.3 us
    convert_element_type x1, other arithmetic, local(): grad_b = (grad_hidden * silu).astype(BF)  26.9 us
    all_gather x1, waiting for transfers between devices, local(): lax.all_gather(expert_part, 'dp', axis=0, tiled=True, axis_index_groups=o...  17.1 us
  transfers between devices with their start and end apart: 38, of which 14 were waited for; matrix products, arithmetic and copies ran while one was open for 34% of the time, Pallas kernels for 0%

profile of v1, /device:TPU:0, one launch (start us, length us, event | category | flops | bytes accessed | tf_op | source)
XLA Modules:
  0.0 740.0 jit_solution(14830488048342055749)
XLA Ops:
  11.3 3.0 collective-permute-start.17
  20.4 3.7 all-to-all-start
  27.1 15.0 %collective-permute-done.19 = bf16[512,1024]{1,0:T(8,128)(2,1)} collective-permute-done((bf16[512,1024]{1,0:T(8,128)(2,1)}, bf16[512,1024]{1,0:T(8,128)(2,1)}, u32[]{:S(2)}, u32[]{:S(2)}) %collective-permute-start.19) | collective-permute-done | bytes 1048608 | tf_op jit(solution)/shard_map/ppermute | solution.py:88
  44.0 4.5 collective-permute-start.21
  50.4 3.2 collective-permute-start.22
  56.0 8.2 %all-to-all-done = bf16[8,32,3072]{2,1,0:T(8,128)(2,1)S(1)} async-done(((bf16[8,32,3072]{2,1,0:T(8,128)(2,1)}), bf16[8,32,3072]{2,1,0:T(8,128)(2,1)S(1)}, u32[]{:S(2)}, u32[]{:S(2)}) %all-to-all-start) | async-done | bytes 1572896 | tf_op jit(solution)/shard_map/all_to_all | solution.py:158
  65.4 14.5 %collective-permute-done.21 = bf16[256,1024]{1,0:T(8,128)(2,1)S(1)} collective-permute-done((bf16[256,1024]{1,0:T(8,128)(2,1)}, bf16[256,1024]{1,0:T(8,128)(2,1)S(1)}, u32[]{:S(2)}, u32[]{:S(2)}) %collective-permute-start.21) | collective-permute-done | bytes 524320 | tf_op jit(solution)/shard_map/ppermute | solution.py:88
  82.0 14.3 %all-gather.3.cloned.1.call-done = bf16[1024,3200]{1,0:T(8,128)(2,1)} async-done(((bf16[32,3200]{1,0:T(8,128)(2,1)}), bf16[1024,3200]{1,0:T(8,128)(2,1)}) %all-gather.3.cloned.1.call-update) | async-done | bytes 6553616 | tf_op jit(solution)/shard_map/all_gather | solution.py:144
  97.8 3.0 fusion.22
  103.9 7.9 %fusion.102 = (f32[8,2,512]{2,1,0:T(2,128)S(1)}, f32[8,2,512,512]{2,3,1,0:T(8,128)}) fusion(bf16[512,8,2,32]{0,3,2,1:T(8,128)(2,1)S(1)} %bitcast.218, bf16[512,8,2,32]{0,3,2,1:T(8,128)(2,1)S(1)} %bitcast.216, bf16[512,8,32]{0,2,1:T(8,128)(2,1)S(1)} %get-tuple-element.117, bf16[512,8,32]{0,2,1:T(8,128)(2,1)S(1)} %get-tuple-element.116, ...), kind=kOutput, calls=%fused_computation.255 | convolution fusion | flops 552591360 | bytes 18644992 | tf_op jit(solution)/shard_map/qgrd,kgd->grqk/dot_general | solution.py:60
  111.9 8.3 %fusion.5 = f32[8,2,512]{2,1,0:T(2,128)S(1)} fusion(f32[8,2,512,512]{2,3,1,0:T(8,128)} %get-tuple-element.145, f32[8,2,512]{2,1,0:T(2,128)S(1)} %get-tuple-element.144), kind=kLoop, calls=%fused_computation.20 | loop fusion | flops 8380416 | bytes 16842752 | tf_op jit(solution)/shard_map/reduce_sum | solution.py:64
  122.3 7.8 %fusion.40 = bf16[8,64,2,512]{3,1,2,0:T(8,128)(2,1)S(1)} fusion(bf16[512,8,64,1]{0,2,3,1:T(8,128)(2,1)S(1)} %bitcast.227, f32[8,2,512,512]{2,3,1,0:T(8,128)} %get-tuple-element.145, f32[8,2,512]{2,1,0:T(2,128)S(1)} %fusion.5, f32[8,2,512]{2,1,0:T(2,128)S(1)} %get-tuple-element.144), kind=kOutput, calls=%fused_computation.82 | convolution fusion | flops 549978112 | bytes 18415616 | tf_op jit(solution)/shard_map/grqk,kgd->qgrd/dot_general | solution.py:66
  130.1 3.4 multiply_reduce_fusion.2
  159.5 7.1 collective-permute-done.3
  172.7 7.5 %collective-permute-done.5 = bf16[264,1024]{1,0:T(8,128)(2,1)} collective-permute-done((bf16[264,1024]{1,0:T(8,128)(2,1)S(1)}, bf16[264,1024]{1,0:T(8,128)(2,1)}, u32[]{:S(2)}, u32[]{:S(2)}) %collective-permute-start.5) | collective-permute-done | bytes 540704 | tf_op jit(solution)/shard_map/ppermute | solution.py:88
  181.3 2.9 collective-permute-done.6
  196.0 17.1 %all-gather.5.cloned.1.call-done = bf16[1024,3072]{1,0:T(8,128)(2,1)} async-done(((bf16[256,3072]{1,0:T(8,128)(2,1)}), bf16[1024,3072]{1,0:T(8,128)(2,1)}) %all-gather.5.cloned.1.call-update) | async-done | bytes 6291472 | tf_op jit(solution)/shard_map/all_gather | solution.py:161
  213.2 16.7 %fusion.28 = f32[4096,1024]{0,1:T(8,128)} fusion(bf16[4096,1024]{1,0:T(8,128)(2,1)} %slice_dynamic-update-slice_fusion, bf16[1024,3072]{1,0:T(8,128)(2,1)} %all-gather.5.cloned.1.call-done), kind=kOutput, calls=%fused_computation.70 | convolution fusion | flops 8589934592 | bytes 27262976 | tf_op jit(solution)/shard_map/dot_general | solution.py:22
  229.9 14.3 %fusion.32 = f32[4096,1024]{0,1:T(8,128)} fusion(bf16[4096,1024]{1,0:T(8,128)(2,1)S(1)} %copy-done.39, bf16[1024,3072]{1,0:T(8,128)(2,1)} %all-gather.5.cloned.1.call-done), kind=kOutput, calls=%fused_computation.74 | convolution fusion | flops 8589934592 | bytes 27262976 | tf_op jit(solution)/shard_map/dot_general | solution.py:22
  244.2 29.7 %bitcast_reduce_fusion = (f32[4096,2]{0,1:T(2,128)S(1)}, bf16[4096,1024]{0,1:T(8,128)(2,1)}, f32[4096,1024]{0,1:T(8,128)}) fusion(f32[4096,1024]{0,1:T(8,128)} %fusion.28, f32[4096,1024]{0,1:T(8,128)} %fusion.32, bf16[4096,1024]{1,0:T(8,128)(2,1)} %constant_dynamic-update-slice_fusion.11, bf16[1024,3072]{1,0:T(8,128)(2,1)} %all-gather.5.cloned.1.call-done), kind=kOutput, calls=%fused_computation.9 | convolution fusion | flops 8627675136 | bytes 69238784 | tf_op jit(solution)/shard_map/dot_general | solution.py:22
  274.0 26.9 %multiply_convert_fusion = (bf16[4096,1024]{0,1:T(8,128)(2,1)S(1)}, bf16[4096,1024]{0,1:T(8,128)(2,1)}, bf16[4096,1024]{0,1:T(8,128)(2,1)}) fusion(f32[4096,1024]{0,1:T(8,128)} %get-tuple-element.150, f32[4096,2]{0,1:T(2,128)S(1)} %bitcast.242, f32[4096,1024]{0,1:T(8,128)} %fusion.32, f32[4096,1024]{0,1:T(8,128)} %fusion.28, ...), kind=kLoop, calls=%fused_computation.13 | loop fusion | flops 71303168 | bytes 83918848 | tf_op jit(solution)/shard_map/convert_element_type | solution.py:224
  300.9 14.3 %convolution_convert_fusion.3 = bf16[1024,1024]{0,1:T(8,128)(2,1)S(1)} fusion(bf16[4096,1024]{0,1:T(8,128)(2,1)S(1)} %get-tuple-element.88, bf16[4096,1024]{1,0:T(8,128)(2,1)} %slice_dynamic-update-slice_fusion), kind=kOutput, calls=%fused_computation.63 | convolution fusion | flops 8590983168 | bytes 18874368 | tf_op jit(solution)/shard_map/dot_general | solution.py:22
  315.2 11.6 %convolution_convert_fusion.4 = bf16[1024,1024]{0,1:T(8,128)(2,1)S(1)} fusion(bf16[4096,1024]{0,1:T(8,128)(2,1)S(1)} %copy-done.6, bf16[4096,1024]{1,0:T(8,128)(2,1)} %slice_dynamic-update-slice_fusion), kind=kOutput, calls=%fused_computation.64 | convolution fusion | flops 8590983168 | bytes 18874368 | tf_op jit(solution)/shard_map/dot_general | solution.py:22
  326.8 11.2 %convolution_convert_fusion.2 = bf16[1024,1024]{0,1:T(8,128)(2,1)S(1)} fusion(bf16[4096,1024]{0,1:T(8,128)(2,1)S(1)} %bitcast.212, bf16[4096,1024]{1,0:T(8,128)(2,1)} %constant_dynamic-update-slice_fusion.11), kind=kOutput, calls=%fused_computation.62 | convolution fusion | flops 8590983168 | bytes 18874368 | tf_op jit(solution)/shard_map/dot_general | solution.py:22
  338.0 13.3 %pad_maximum_fusion = bf16[1024,3072]{0,1:T(8,128)(2,1)} fusion(bf16[1024,1024]{0,1:T(8,128)(2,1)S(1)} %convolution_convert_fusion.2, bf16[1024,1024]{0,1:T(8,128)(2,1)S(1)} %convolution_convert_fusion.3, bf16[1024,1024]{0,1:T(8,128)(2,1)S(1)} %convolution_convert_fusion.4), kind=kLoop, calls=%fused_computation.26 | loop fusion | flops 18874368 | bytes 12582912 | tf_op jit(solution)/shard_map/concatenate | solution.py:249
  351.5 13.5 %convolution_convert_fusion = bf16[4096,1024]{1,0:T(8,128)(2,1)S(1)} fusion(bf16[4096,1024]{0,1:T(8,128)(2,1)} %get-tuple-element.136, bf16[1024,3072]{1,0:T(8,128)(2,1)} %all-gather.5.cloned.1.call-done), kind=kOutput, calls=%fused_computation.25 | convolution fusion | flops 8594128896 | bytes 18874368 | tf_op jit(solution)/shard_map/dot_general | solution.py:22
  369.3 16.3 %fusion.30 = f32[4096,1024]{1,0:T(8,128)} fusion(bf16[4096,1024]{0,1:T(8,128)(2,1)} %get-tuple-element.89, bf16[1024,3072]{1,0:T(8,128)(2,1)} %all-gather.5.cloned.1.call-done), kind=kOutput, calls=%fused_computation.72 | convolution fusion | flops 8589934592 | bytes 27262976 | tf_op jit(solution)/shard_map/dot_general | solution.py:22
  385.5 17.4 %add_convert_fusion = bf16[4096,1024]{1,0:T(8,128)(2,1)} fusion(f32[4096,1024]{1,0:T(8,128)} %fusion.30, bf16[4096,1024]{0,1:T(8,128)(2,1)} %copy-done.5, bf16[1024,3072]{1,0:T(8,128)(2,1)} %all-gather.5.cloned.1.call-done), kind=kOutput, calls=%fused_computation.12 | convolution fusion | flops 8598323200 | bytes 35651584 | tf_op jit(solution)/shard_map/dot_general | solution.py:22
  403.0 4.1 fusion.96
  408.7 3.3 convert_add_fusion.5
  417.2 20.8 %collective-permute-done.27 = bf16[264,1024]{1,0:T(8,128)(2,1)S(1)} collective-permute-done((bf16[264,1024]{1,0:T(8,128)(2,1)S(1)}, bf16[264,1024]{1,0:T(8,128)(2,1)S(1)}, u32[]{:S(2)}, u32[]{:S(2)}) %collective-permute-start.27) | collective-permute-done | bytes 540704 | tf_op jit(solution)/shard_map/ppermute | solution.py:88
  443.6 31.5 %collective-permute-done.14 = bf16[256,1024]{1,0:T(8,128)(2,1)S(1)} collective-permute-done((bf16[256,1024]{1,0:T(8,128)(2,1)S(1)}, bf16[256,1024]{1,0:T(8,128)(2,1)S(1)}, u32[]{:S(2)}, u32[]{:S(2)}) %collective-permute-start.14) | collective-permute-done | bytes 524320 | tf_op jit(solution)/shard_map/ppermute | solution.py:88
  483.5 3.1 multiply_reduce_fusion
  486.7 12.6 %collective-permute-done.12 = bf16[512,1024]{1,0:T(8,128)(2,1)} collective-permute-done((bf16[512,1024]{1,0:T(8,128)(2,1)}, bf16[512,1024]{1,0:T(8,128)(2,1)}, u32[]{:S(2)}, u32[]{:S(2)}) %collective-permute-start.12) | collective-permute-done | bytes 1048608 | tf_op jit(solution)/shard_map/ppermute | solution.py:88
  501.7 4.2 subtract_add_fusion
  510.7 13.7 %fusion.1 = (f32[8,2,512]{2,1,0:T(2,128)S(1)}, f32[8,512,512,2]{2,1,3,0:T(8,128)}) fusion(f32[8,2,512,512]{2,3,1,0:T(8,128)} %get-tuple-element.145, f32[8,2,512]{2,1,0:T(2,128)S(1)} %bitcast.236, bf16[512,8,64,1]{0,2,3,1:T(8,128)(2,1)} %bitcast.228, bf16[512,8,2,64]{0,3,2,1:T(8,128)(2,1)S(1)} %bitcast.209), kind=kOutput, calls=%fused_computation.6 | convolution fusion | flops 549445632 | bytes 35192832 | tf_op jit(solution)/shard_map/qgrd,kgd->grqk/dot_general | solution.py:74
  527.3 11.2 %fusion.3 = bf16[8,2,512,512]{2,3,1,0:T(8,128)(2,1)} fusion(f32[8,512,512,2]{2,1,3,0:T(8,128)} %get-tuple-element.153, f32[8,2,512,512]{2,3,1,0:T(8,128)S(1)} %bitcast.208, f32[8,2,512]{2,1,0:T(2,128)S(1)} %get-tuple-element.152, f32[8,2,512]{2,1,0:T(2,128)S(1)} %bitcast.237), kind=kLoop, calls=%fused_computation.8 | loop fusion | flops 16777216 | bytes 42008576 | tf_op jit(solution)/shard_map/convert_element_type | solution.py:76
  538.5 6.0 fusion.48
  545.6 4.9 convolution_multiply_fusion
  551.9 3.5 fusion.49
  555.5 6.9 fusion.21
  566.9 4.6 convolution_convert_fusion.1
  572.3 10.9 %concatenate.133 = bf16[1024,3200]{1,0:T(8,128)(2,1)} concatenate(bf16[1024,2048]{1,0:T(8,128)(2,1)} %convolution_convert_fusion.1, bf16[1024,1024]{1,0:T(8,128)(2,1)} %convolution_convert_fusion.5, bf16[1024,16]{1,0:T(8,128)(2,1)S(1)} %copy.180, bf16[1024,1]{1,0:T(8,128)(2,1)} %broadcast_in_dim.82, bf16[1024,1]{1,0:T(8,128)(2,1)} %broadcast_in_dim.83, ...), dimensions={1} | concatenate | bytes 13107200 | tf_op jit(solution)/shard_map/concatenate | solution.py:290
  585.8 4.7 all-to-all-start.1
  590.5 3.5 fusion.18
  594.0 32.9 %all-to-all-done.1 = bf16[8,32,3072]{2,1,0:T(8,128)(2,1)} async-done(((bf16[8,32,3072]{2,1,0:T(8,128)(2,1)}), bf16[8,32,3072]{2,1,0:T(8,128)(2,1)}, u32[]{:S(2)}, u32[]{:S(2)}) %all-to-all-start.1) | async-done | bytes 1572896 | tf_op jit(solution)/shard_map/all_to_all | solution.py:253
  626.9 4.0 reshape.281
  636.2 90.2 %reduce-scatter.3.cloned.1.call-done = bf16[32,3200]{1,0:T(8,128)(2,1)} async-done(((bf16[1024,3200]{1,0:T(8,128)(2,1)}), bf16[32,3200]{1,0:T(8,128)(2,1)}) %reduce-scatter.3.cloned.1.call-update) | async-done | bytes 204816 | tf_op jit(solution)/shard_map/reduce_scatter | solution.py:301
  (337 shorter events, 130.9 us)
Async XLA Ops:
  7.2 89.2 %all-gather.3.cloned.1.call-start = ((), (), s32[]{:S(2)}) async-start(), calls=%async_computation.4 | async-start | bytes 6758400 | tf_op jit(solution)/shard_map/all_gather | solution.py:144
  11.3 37.2 %collective-permute-start.17 = (bf16[512,1024]{1,0:T(8,128)(2,1)}, bf16[512,1024]{1,0:T(8,128)(2,1)}, u32[]{:S(2)}, u32[]{:S(2)}) collective-permute-start(bf16[512,1024]{1,0:T(8,128)(2,1)} %param.27), channel_id=1, source_target_pairs={{0,2},{1,3},{2,0},{3,1},{4,6},{5,7},{6,4},{7,5},{8,10},{9,11},{10,... | collective-permute-start | bytes 3145736 | tf_op jit(solution)/shard_map/ppermute | solution.py:88
  14.3 27.9 %collective-permute-start.19 = (bf16[512,1024]{1,0:T(8,128)(2,1)}, bf16[512,1024]{1,0:T(8,128)(2,1)}, u32[]{:S(2)}, u32[]{:S(2)}) collective-permute-start(bf16[512,1024]{1,0:T(8,128)(2,1)} %param.27), channel_id=1, source_target_pairs={{0,4},{1,5},{2,6},{3,7},{4,0},{5,1},{6,2},{7,3},{8,12},{9,13},{10,... | collective-permute-start | bytes 3145736 | tf_op jit(solution)/shard_map/ppermute | solution.py:88
  20.4 43.7 %all-to-all-start = ((bf16[8,32,3072]{2,1,0:T(8,128)(2,1)}), bf16[8,32,3072]{2,1,0:T(8,128)(2,1)S(1)}, u32[]{:S(2)}, u32[]{:S(2)}) async-start(bf16[8,32,3072]{2,1,0:T(8,128)(2,1)} %copy.164), calls=%async_computation | async-start | bytes 3145728 | tf_op jit(solution)/shard_map/all_to_all | solution.py:158
  24.1 189.0 %all-gather.5.cloned.1.call-start = ((), (), s32[]{:S(2)}) async-start(), calls=%async_computation.5 | async-start | bytes 7864320 | tf_op jit(solution)/shard_map/all_gather | solution.py:161
  24.2 114.8 %collective-permute-start.16 = (bf16[512,1024]{1,0:T(8,128)(2,1)S(1)}, bf16[512,1024]{1,0:T(8,128)(2,1)}, u32[]{:S(2)}, u32[]{:S(2)}) collective-permute-start(bf16[512,1024]{1,0:T(8,128)(2,1)S(1)} %copy-done.11), channel_id=1, source_target_pairs={{0,1},{1,0},{2,3},{3,2},{4,5},{5,4},{6,7},{7,6},{8,9},{9,8},{10,11... | collective-permute-start | bytes 3145736 | tf_op jit(solution)/shard_map/ppermute | solution.py:88
  26.2 28.3 %copy-start.49 = (s32[1,512]{1,0:T(1,128)S(1)}, s32[1,512]{1,0:T(1,128)}, u32[]{:S(2)}) copy-start(s32[1,512]{1,0:T(1,128)} %param.26) | copy-start | bytes 6148
  27.1 93.0 %copy-start.52 = (f32[512]{0:T(512)}, f32[512]{0:T(512)S(1)}, u32[]{:S(2)}) copy-start(f32[512]{0:T(512)S(1)} %get-tuple-element.138) | copy-start | bytes 6148
  44.0 36.0 %collective-permute-start.21 = (bf16[256,1024]{1,0:T(8,128)(2,1)}, bf16[256,1024]{1,0:T(8,128)(2,1)S(1)}, u32[]{:S(2)}, u32[]{:S(2)}) collective-permute-start(bf16[256,1024]{1,0:T(8,128)(2,1)} %slice.476), channel_id=1, source_target_pairs={{0,2},{1,3},{2,0},{3,1},{4,6},{5,7},{6,4},{7,5},{8,10},{9,11},{10,... | collective-permute-start | bytes 1572872 | tf_op jit(solution)/shard_map/ppermute | solution.py:88
  50.4 29.6 %collective-permute-start.22 = (bf16[256,1024]{1,0:T(8,128)(2,1)}, bf16[256,1024]{1,0:T(8,128)(2,1)}, u32[]{:S(2)}, u32[]{:S(2)}) collective-permute-start(bf16[256,1024]{1,0:T(8,128)(2,1)} %slice.477), channel_id=1, source_target_pairs={{0,4},{1,5},{2,6},{3,7},{4,0},{5,1},{6,2},{7,3},{8,12},{9,13},{10,... | collective-permute-start | bytes 1572872 | tf_op jit(solution)/shard_map/ppermute | solution.py:88
  54.6 49.1 %copy-start.20 = (f32[512,32]{0,1:T(8,128)}, f32[512,32]{0,1:T(8,128)S(1)}, u32[]{:S(2)}) copy-start(f32[512,32]{0,1:T(8,128)S(1)} %get-tuple-element.143) | copy-start | bytes 196612
  55.5 85.1 %collective-permute-start.18 = (bf16[512,1024]{1,0:T(8,128)(2,1)}, bf16[512,1024]{1,0:T(8,128)(2,1)}, u32[]{:S(2)}, u32[]{:S(2)}) collective-permute-start(bf16[512,1024]{1,0:T(8,128)(2,1)} %collective-permute-done.17), channel_id=1, source_target_pairs={{0,1},{1,0},{2,3},{3,2},{4,5},{5,4},{6,7},{7,6},{8,9},{9,8},{10,11... | collective-permute-start | bytes 3145736 | tf_op jit(solution)/shard_map/ppermute | solution.py:88
  55.5 95.9 %collective-permute-start.20 = (bf16[512,1024]{1,0:T(8,128)(2,1)}, bf16[512,1024]{1,0:T(8,128)(2,1)}, u32[]{:S(2)}, u32[]{:S(2)}) collective-permute-start(bf16[512,1024]{1,0:T(8,128)(2,1)} %collective-permute-done.19), channel_id=1, source_target_pairs={{0,1},{1,0},{2,3},{3,2},{4,5},{5,4},{6,7},{7,6},{8,9},{9,8},{10,11... | collective-permute-start | bytes 3145736 | tf_op jit(solution)/shard_map/ppermute | solution.py:88
  65.4 32.5 %copy-start.14 = (bf16[512,1024]{1,0:T(8,128)(2,1)S(1)}, bf16[512,1024]{1,0:T(8,128)(2,1)}, u32[]{:S(2)}) copy-start(bf16[512,1024]{1,0:T(8,128)(2,1)} %param.14) | copy-start | bytes 3145732
  65.4 517.8 %reduce-scatter.5.cloned.1.call-start = ((), (), s32[]{:S(2)}) async-start(), calls=%async_computation.7 | async-start | bytes 7864320 | tf_op jit(solution)/shard_map/reduce_scatter | solution.py:250
  82.0 74.3 %collective-permute-start.23 = (bf16[512,1024]{1,0:T(8,128)(2,1)}, bf16[512,1024]{1,0:T(8,128)(2,1)}, u32[]{:S(2)}, u32[]{:S(2)}) collective-permute-start(bf16[512,1024]{1,0:T(8,128)(2,1)} %pad_maximum_fusion.11), channel_id=1, source_target_pairs={{0,1},{1,0},{2,3},{3,2},{4,5},{5,4},{6,7},{7,6},{8,9},{9,8},{10,11... | collective-permute-start | bytes 3145736 | tf_op jit(solution)/shard_map/ppermute | solution.py:88
  97.8 22.3 %copy-start.46 = (f32[1024]{0:T(1024)}, f32[1024]{0:T(1024)S(1)}, u32[]{:S(2)}) copy-start(f32[1024]{0:T(1024)S(1)} %get-tuple-element.73) | copy-start | bytes 12292
  97.8 36.3 %copy-start.40 = (f32[1024]{0:T(1024)}, f32[1024]{0:T(1024)S(1)}, u32[]{:S(2)}) copy-start(f32[1024]{0:T(1024)S(1)} %get-tuple-element.72) | copy-start | bytes 12292
  138.7 20.0 %collective-permute-start = (bf16[528,1024]{1,0:T(8,128)(2,1)}, bf16[528,1024]{1,0:T(8,128)(2,1)}, u32[]{:S(2)}, u32[]{:S(2)}) collective-permute-start(bf16[528,1024]{1,0:T(8,128)(2,1)} %maximum_maximum_fusion), channel_id=1, source_target_pairs={{0,1},{1,0},{2,3},{3,2},{4,5},{5,4},{6,7},{7,6},{8,9},{9,8},{10,11... | collective-permute-start | bytes 3244040 | tf_op jit(solution)/shard_map/ppermute | solution.py:88
  139.0 28.1 %collective-permute-start.1 = (bf16[528,1024]{1,0:T(8,128)(2,1)}, bf16[528,1024]{1,0:T(8,128)(2,1)S(1)}, u32[]{:S(2)}, u32[]{:S(2)}) collective-permute-start(bf16[528,1024]{1,0:T(8,128)(2,1)} %maximum_maximum_fusion), channel_id=1, source_target_pairs={{0,2},{1,3},{2,0},{3,1},{4,6},{5,7},{6,4},{7,5},{8,10},{9,11},{10,... | collective-permute-start | bytes 3244040 | tf_op jit(solution)/shard_map/ppermute | solution.py:88
  140.6 26.0 %collective-permute-start.3 = (bf16[528,1024]{1,0:T(8,128)(2,1)}, bf16[528,1024]{1,0:T(8,128)(2,1)S(1)}, u32[]{:S(2)}, u32[]{:S(2)}) collective-permute-start(bf16[528,1024]{1,0:T(8,128)(2,1)} %maximum_maximum_fusion), channel_id=1, source_target_pairs={{0,4},{1,5},{2,6},{3,7},{4,0},{5,1},{6,2},{7,3},{8,12},{9,13},{10,... | collective-permute-start | bytes 3244040 | tf_op jit(solution)/shard_map/ppermute | solution.py:88
  166.6 13.6 %collective-permute-start.5 = (bf16[264,1024]{1,0:T(8,128)(2,1)S(1)}, bf16[264,1024]{1,0:T(8,128)(2,1)}, u32[]{:S(2)}, u32[]{:S(2)}) collective-permute-start(bf16[264,1024]{1,0:T(8,128)(2,1)S(1)} %slice.432), channel_id=1, source_target_pairs={{0,2},{1,3},{2,0},{3,1},{4,6},{5,7},{6,4},{7,5},{8,10},{9,11},{10,... | collective-permute-start | bytes 1622024 | tf_op jit(solution)/shard_map/ppermute | solution.py:88
  167.0 18.1 %collective-permute-start.4 = (bf16[528,1024]{1,0:T(8,128)(2,1)S(1)}, bf16[528,1024]{1,0:T(8,128)(2,1)}, u32[]{:S(2)}, u32[]{:S(2)}) collective-permute-start(bf16[528,1024]{1,0:T(8,128)(2,1)S(1)} %collective-permute-done.3), channel_id=1, source_target_pairs={{0,1},{1,0},{2,3},{3,2},{4,5},{5,4},{6,7},{7,6},{8,9},{9,8},{10,11... | collective-permute-start | bytes 3244040 | tf_op jit(solution)/shard_map/ppermute | solution.py:88
  167.0 17.3 %collective-permute-start.2 = (bf16[528,1024]{1,0:T(8,128)(2,1)S(1)}, bf16[528,1024]{1,0:T(8,128)(2,1)}, u32[]{:S(2)}, u32[]{:S(2)}) collective-permute-start(bf16[528,1024]{1,0:T(8,128)(2,1)S(1)} %collective-permute-done.1), channel_id=1, source_target_pairs={{0,1},{1,0},{2,3},{3,2},{4,5},{5,4},{6,7},{7,6},{8,9},{9,8},{10,11... | collective-permute-start | bytes 3244040 | tf_op jit(solution)/shard_map/ppermute | solution.py:88
  170.0 14.2 %collective-permute-start.6 = (bf16[264,1024]{1,0:T(8,128)(2,1)S(1)}, bf16[264,1024]{1,0:T(8,128)(2,1)S(1)}, u32[]{:S(2)}, u32[]{:S(2)}) collective-permute-start(bf16[264,1024]{1,0:T(8,128)(2,1)S(1)} %slice.433), channel_id=1, source_target_pairs={{0,4},{1,5},{2,6},{3,7},{4,0},{5,1},{6,2},{7,3},{8,12},{9,13},{10,... | collective-permute-start | bytes 1622024 | tf_op jit(solution)/shard_map/ppermute | solution.py:88
  184.3 8.6 %collective-permute-start.7 = (bf16[528,1024]{1,0:T(8,128)(2,1)S(1)}, bf16[528,1024]{1,0:T(8,128)(2,1)}, u32[]{:S(2)}, u32[]{:S(2)}) collective-permute-start(bf16[528,1024]{1,0:T(8,128)(2,1)S(1)} %constant_dynamic-update-slice_fusion), channel_id=1, source_target_pairs={{0,1},{1,0},{2,3},{3,2},{4,5},{5,4},{6,7},{7,6},{8,9},{9,8},{10,11... | collective-permute-start | bytes 3244040 | tf_op jit(solution)/shard_map/ppermute | solution.py:88
  213.2 16.8 %copy-start.39 = (bf16[4096,1024]{1,0:T(8,128)(2,1)S(1)}, bf16[4096,1024]{1,0:T(8,128)(2,1)}, u32[]{:S(2)}) copy-start(bf16[4096,1024]{1,0:T(8,128)(2,1)} %slice_dynamic-update-slice_fusion) | copy-start | bytes 25165828
  300.9 25.9 %slice-start.4 = ((s8[8388608]{0:T(1024)(128)(4,1)}), s8[4194304]{0:T(1024)(128)(4,1)S(1)}, s32[]{:S(2)}) async-start(s8[8388608]{0:T(1024)(128)(4,1)} %bitcast.211), calls=%async_computation.12 | async-start | bytes 8388608
  351.4 375.0 %reduce-scatter.3.cloned.1.call-start = ((), (), s32[]{:S(2)}) async-start(), calls=%async_computation.6 | async-start | bytes 6758400 | tf_op jit(solution)/shard_map/reduce_scatter | solution.py:301
  368.6 39.4 %collective-permute-start.10 = (bf16[512,1024]{1,0:T(8,128)(2,1)S(1)}, bf16[512,1024]{1,0:T(8,128)(2,1)S(1)}, u32[]{:S(2)}, u32[]{:S(2)}) collective-permute-start(bf16[512,1024]{1,0:T(8,128)(2,1)S(1)} %get-tuple-element.100), channel_id=1, source_target_pairs={{0,1},{1,0},{2,3},{3,2},{4,5},{5,4},{6,7},{7,6},{8,9},{9,8},{10,11... | collective-permute-start | bytes 3145736 | tf_op jit(solution)/shard_map/ppermute | solution.py:88
  368.7 39.9 %collective-permute-start.13 = (bf16[512,1024]{1,0:T(8,128)(2,1)S(1)}, bf16[512,1024]{1,0:T(8,128)(2,1)S(1)}, u32[]{:S(2)}, u32[]{:S(2)}) collective-permute-start(bf16[512,1024]{1,0:T(8,128)(2,1)S(1)} %get-tuple-element.99), channel_id=1, source_target_pairs={{0,1},{1,0},{2,3},{3,2},{4,5},{5,4},{6,7},{7,6},{8,9},{9,8},{10,11... | collective-permute-start | bytes 3145736 | tf_op jit(solution)/shard_map/ppermute | solution.py:88
  369.1 39.5 %collective-permute-start.9 = (bf16[512,1024]{1,0:T(8,128)(2,1)S(1)}, bf16[512,1024]{1,0:T(8,128)(2,1)S(1)}, u32[]{:S(2)}, u32[]{:S(2)}) collective-permute-start(bf16[512,1024]{1,0:T(8,128)(2,1)S(1)} %get-tuple-element.101), channel_id=1, source_target_pairs={{0,1},{1,0},{2,3},{3,2},{4,5},{5,4},{6,7},{7,6},{8,9},{9,8},{10,11... | collective-permute-start | bytes 3145736 | tf_op jit(solution)/shard_map/ppermute | solution.py:88
  407.1 6.4 collective-permute-start.26
  407.8 70.0 %collective-permute-start.24 = (bf16[528,1024]{1,0:T(8,128)(2,1)S(1)}, bf16[528,1024]{1,0:T(8,128)(2,1)S(1)}, u32[]{:S(2)}, u32[]{:S(2)}) collective-permute-start(bf16[528,1024]{1,0:T(8,128)(2,1)S(1)} %pad_maximum_fusion.2), channel_id=1, source_target_pairs={{0,1},{1,0},{2,3},{3,2},{4,5},{5,4},{6,7},{7,6},{8,9},{9,8},{10,11... | collective-permute-start | bytes 3244040 | tf_op jit(solution)/shard_map/ppermute | solution.py:88
  408.0 6.7 collective-permute-start.25
  408.6 8.0 %collective-permute-start.29 = (bf16[528,1024]{1,0:T(8,128)(2,1)S(1)}, bf16[528,1024]{1,0:T(8,128)(2,1)S(1)}, u32[]{:S(2)}, u32[]{:S(2)}) collective-permute-start(bf16[528,1024]{1,0:T(8,128)(2,1)S(1)} %pad_maximum_fusion.6), channel_id=1, source_target_pairs={{0,1},{1,0},{2,3},{3,2},{4,5},{5,4},{6,7},{7,6},{8,9},{9,8},{10,11... | collective-permute-start | bytes 3244040 | tf_op jit(solution)/shard_map/ppermute | solution.py:88
  412.0 30.2 %collective-permute-start.11 = (bf16[256,1024]{1,0:T(8,128)(2,1)S(1)}, bf16[256,1024]{1,0:T(8,128)(2,1)S(1)}, u32[]{:S(2)}, u32[]{:S(2)}) collective-permute-start(bf16[256,1024]{1,0:T(8,128)(2,1)S(1)} %get-tuple-element.120), channel_id=1, source_target_pairs={{0,4},{1,5},{2,6},{3,7},{4,0},{5,1},{6,2},{7,3},{8,12},{9,13},{10,... | collective-permute-start | bytes 1572872 | tf_op jit(solution)/shard_map/ppermute | solution.py:88
  414.1 23.9 %collective-permute-start.27 = (bf16[264,1024]{1,0:T(8,128)(2,1)S(1)}, bf16[264,1024]{1,0:T(8,128)(2,1)S(1)}, u32[]{:S(2)}, u32[]{:S(2)}) collective-permute-start(bf16[264,1024]{1,0:T(8,128)(2,1)S(1)} %get-tuple-element.118), channel_id=1, source_target_pairs={{0,4},{1,5},{2,6},{3,7},{4,0},{5,1},{6,2},{7,3},{8,12},{9,13},{10,... | collective-permute-start | bytes 1622024 | tf_op jit(solution)/shard_map/ppermute | solution.py:88
  414.7 25.0 %collective-permute-start.30 = (bf16[264,1024]{1,0:T(8,128)(2,1)S(1)}, bf16[264,1024]{1,0:T(8,128)(2,1)S(1)}, u32[]{:S(2)}, u32[]{:S(2)}) collective-permute-start(bf16[264,1024]{1,0:T(8,128)(2,1)S(1)} %get-tuple-element.119), channel_id=1, source_target_pairs={{0,2},{1,3},{2,0},{3,1},{4,6},{5,7},{6,4},{7,5},{8,10},{9,11},{10,... | collective-permute-start | bytes 1622024 | tf_op jit(solution)/shard_map/ppermute | solution.py:88
  438.2 40.9 %collective-permute-start.28 = (bf16[528,1024]{1,0:T(8,128)(2,1)S(1)}, bf16[528,1024]{1,0:T(8,128)(2,1)S(1)}, u32[]{:S(2)}, u32[]{:S(2)}) collective-permute-start(bf16[528,1024]{1,0:T(8,128)(2,1)S(1)} %pad_maximum_fusion.5), channel_id=1, source_target_pairs={{0,2},{1,3},{2,0},{3,1},{4,6},{5,7},{6,4},{7,5},{8,10},{9,11},{10,... | collective-permute-start | bytes 3244040 | tf_op jit(solution)/shard_map/ppermute | solution.py:88
  440.0 39.2 %collective-permute-start.31 = (bf16[528,1024]{1,0:T(8,128)(2,1)S(1)}, bf16[528,1024]{1,0:T(8,128)(2,1)S(1)}, u32[]{:S(2)}, u32[]{:S(2)}) collective-permute-start(bf16[528,1024]{1,0:T(8,128)(2,1)S(1)} %pad_maximum_fusion.7), channel_id=1, source_target_pairs={{0,4},{1,5},{2,6},{3,7},{4,0},{5,1},{6,2},{7,3},{8,12},{9,13},{10,... | collective-permute-start | bytes 3244040 | tf_op jit(solution)/shard_map/ppermute | solution.py:88
  441.5 33.5 %collective-permute-start.14 = (bf16[256,1024]{1,0:T(8,128)(2,1)S(1)}, bf16[256,1024]{1,0:T(8,128)(2,1)S(1)}, u32[]{:S(2)}, u32[]{:S(2)}) collective-permute-start(bf16[256,1024]{1,0:T(8,128)(2,1)S(1)} %get-tuple-element.121), channel_id=1, source_target_pairs={{0,2},{1,3},{2,0},{3,1},{4,6},{5,7},{6,4},{7,5},{8,10},{9,11},{10,... | collective-permute-start | bytes 1572872 | tf_op jit(solution)/shard_map/ppermute | solution.py:88
  442.3 44.4 %collective-permute-start.8 = (bf16[512,1024]{1,0:T(8,128)(2,1)}, bf16[512,1024]{1,0:T(8,128)(2,1)}, u32[]{:S(2)}, u32[]{:S(2)}) collective-permute-start(bf16[512,1024]{1,0:T(8,128)(2,1)} %get-tuple-element.98), channel_id=1, source_target_pairs={{0,1},{1,0},{2,3},{3,2},{4,5},{5,4},{6,7},{7,6},{8,9},{9,8},{10,11... | collective-permute-start | bytes 3145736 | tf_op jit(solution)/shard_map/ppermute | solution.py:88
  475.1 24.2 %collective-permute-start.12 = (bf16[512,1024]{1,0:T(8,128)(2,1)}, bf16[512,1024]{1,0:T(8,128)(2,1)}, u32[]{:S(2)}, u32[]{:S(2)}) collective-permute-start(bf16[512,1024]{1,0:T(8,128)(2,1)} %pad_maximum_fusion.9), channel_id=1, source_target_pairs={{0,2},{1,3},{2,0},{3,1},{4,6},{5,7},{6,4},{7,5},{8,10},{9,11},{10,... | collective-permute-start | bytes 3145736 | tf_op jit(solution)/shard_map/ppermute | solution.py:88
  477.7 24.0 %collective-permute-start.15 = (bf16[512,1024]{1,0:T(8,128)(2,1)}, bf16[512,1024]{1,0:T(8,128)(2,1)}, u32[]{:S(2)}, u32[]{:S(2)}) collective-permute-start(bf16[512,1024]{1,0:T(8,128)(2,1)} %pad_maximum_fusion.10), channel_id=1, source_target_pairs={{0,4},{1,5},{2,6},{3,7},{4,0},{5,1},{6,2},{7,3},{8,12},{9,13},{10,... | collective-permute-start | bytes 3145736 | tf_op jit(solution)/shard_map/ppermute | solution.py:88
  483.5 18.2 %copy-start.12 = (bf16[512,1024]{1,0:T(8,128)(2,1)S(1)}, bf16[512,1024]{1,0:T(8,128)(2,1)}, u32[]{:S(2)}) copy-start(bf16[512,1024]{1,0:T(8,128)(2,1)} %param.27) | copy-start | bytes 3145732
  483.5 18.2 %copy-start.54 = (f32[512]{0:T(512)S(1)}, f32[512]{0:T(512)}, u32[]{:S(2)}) copy-start(f32[512]{0:T(512)} %get-tuple-element.139) | copy-start | bytes 6148
  585.8 41.1 %all-to-all-start.1 = ((bf16[8,32,3072]{2,1,0:T(8,128)(2,1)}), bf16[8,32,3072]{2,1,0:T(8,128)(2,1)}, u32[]{:S(2)}, u32[]{:S(2)}) async-start(bf16[8,32,3072]{2,1,0:T(8,128)(2,1)} %bitcast.215), calls=%async_computation.3 | async-start | bytes 3145728 | tf_op jit(solution)/shard_map/all_to_all | solution.py:253
  (53 other events, 315.1 us)
Sparse Core Ops, SparseCore 0:
  11.4 84.9 all-gather.2
  98.0 115.1 all-gather.4
  351.5 108.9 reduce-scatter.4
  583.3 143.0 reduce-scatter.2

commit v2 on v1

v2 whole, which is shorter than its diff:
```python
import functools

import jax
import jax.numpy as jnp
from jax import lax
from jax.experimental import pallas as pl
from jax.experimental.pallas import tpu as pltpu
from jax.sharding import PartitionSpec as P

EXPERTS = 16
PLANE = 8
MINE = EXPERTS // PLANE
HEADS = 16
HEAD_SIZE = 64
BLOCK = 128
MOST_DOC = 256
MIB = 2**20
VMEM_ROOM = 60 * MIB
SMALL = pl.CostEstimate(flops=1, bytes_accessed=1, transcendentals=0)
epsilon = 1e-06
neg_large = -1000000000.0
BF = jnp.bfloat16
F32 = jnp.float32


def dot(a, b, ca, cb):
    return lax.dot_general(a, b, (((ca,), (cb,)), ((), ())), preferred_element_type=F32)

def rms_scale(values):
    return lax.rsqrt(jnp.mean(values * values, axis=-1, keepdims=True) + epsilon)

def swap_halves(u):
    lane = lax.broadcasted_iota(jnp.int32, u.shape, 1)
    return jnp.where(lane % 64 < 32, pltpu.roll(u, u.shape[1] - 32, 1), pltpu.roll(u, 32, 1))

def key_range(rows, qb):
    end = (qb + 1) * BLOCK
    return max(0, end - BLOCK - MOST_DOC), end

def fill_mask(mask_ref, seg_col_ref, seg_row_ref, rows):
    for qb in range(rows // BLOCK):
        low, high = key_range(rows, qb)
        keys = low + lax.broadcasted_iota(jnp.int32, (high - low, BLOCK), 0)
        queries = qb * BLOCK + lax.broadcasted_iota(jnp.int32, (high - low, BLOCK), 1)
        same = seg_col_ref[low:high, :1] == seg_row_ref[:1, qb * BLOCK : (qb + 1) * BLOCK]
        mask_ref[qb, : high - low] = jnp.where(same & (keys <= queries), 1.0, 0.0)

def masked_scores(mask_ref, k_c, q_pair, qb, span):
    s = dot(k_c, q_pair, 1, 1)
    m = mask_ref[qb, :span]
    return jnp.where(jnp.concatenate([m, m], axis=1) > 0, s, neg_large)

def piece_copies(me_ref, spots, pieces, whole_ref, sems, inward):
    copies = []
    for ref, (offsets, first) in zip(pieces, spots):
        if offsets is None:
            sides = [(ref, whole_ref)]
        else:
            share, cols = ref.shape[1:]
            sides = []
            for i, offset in enumerate(offsets):
                row = pl.multiple_of((me_ref[0] ^ offset) * share, share)
                sides.append((ref.at[i], whole_ref.at[pl.ds(row, share), first : first + cols]))
        for part, place in sides:
            source, target = (part, place) if inward else (place, part)
            copies.append(pltpu.make_async_copy(source, target, sems.at[len(copies)]))
    return copies


def piece_count(spots):
    return sum(1 if offsets is None else len(offsets) for offsets, _ in spots)


def forward_kernel(spots, me_ref, x_ref, routes_ref, seg_col_ref, seg_row_ref, cos_ref, sin_ref, *refs):
    pieces, refs = refs[: len(spots)], refs[len(spots) :]
    (h1_ref, q_ref, k_ref, v_ref, o_ref, lse_ref, r1_ref, h2_ref, dense_ref) = refs[:9]
    mask_ref, w_ref, sems, out_sem = refs[9:]
    copies = piece_copies(me_ref, spots, pieces, w_ref, sems, True)
    for copy in copies:
        copy.start()
    fill_mask(mask_ref, seg_col_ref, seg_row_ref, x_ref.shape[0])
    for copy in copies:
        copy.wait()
    keep = pltpu.make_async_copy(w_ref, dense_ref, out_sem)
    keep.start()
    rows, width = x_ref.shape
    x = x_ref[...].astype(F32)
    gains = w_ref[:, 3072:3200].astype(F32).T
    h1_ref[...] = (x * rms_scale(x) * gains[16:17]).astype(BF)

    @pl.loop(0, 4)
    def _(j):
        qs = pl.ds(pl.multiple_of(j * 256, 256), 256)
        ks = pl.ds(pl.multiple_of(j * 128, 128), 128)
        vs = pl.ds(pl.multiple_of(1536 + j * 128, 128), 128)
        kw = pl.ds(pl.multiple_of(1024 + j * 128, 128), 128)
        h1 = h1_ref[...]
        cos, sin = cos_ref[...], sin_ref[...]
        q2 = dot(h1, w_ref[:, qs], 1, 0)
        qa, qb_ = q2[:, :128], q2[:, 128:]
        qa = (qa * cos + swap_halves(qa) * sin).astype(BF) * BF(0.125)
        qb_ = (qb_ * cos + swap_halves(qb_) * sin).astype(BF) * BF(0.125)
        k = dot(h1, w_ref[:, kw], 1, 0)
        k = (k * cos + swap_halves(k) * sin).astype(BF)
        v32 = dot(h1, w_ref[:, vs], 1, 0)
        v = v32.astype(BF)
        q_ref[:, qs] = jnp.concatenate([qa, qb_], axis=1)
        k_ref[:, ks] = k
        v_ref[:, ks] = v
        vt = v32.T.astype(BF)
        lane = lax.broadcasted_iota(jnp.int32, (rows, 128), 1)
        sub = lax.broadcasted_iota(jnp.int32, (128, rows), 0)
        outs = []
        for qb in range(rows // BLOCK):
            low, high = key_range(rows, qb)
            blk = slice(qb * BLOCK, (qb + 1) * BLOCK)
            q_pair = jnp.concatenate([qa[blk], qb_[blk]], axis=0)
            total = None
            for c in range(2):
                k_c = jnp.where(lane[low:high] // 64 == c, k[low:high], BF(0))
                vt_c = jnp.where(sub[:, low:high] // 64 == c, vt[:, low:high], BF(0))
                s = masked_scores(mask_ref, k_c, q_pair, qb, high - low)
                top = jnp.max(s, axis=0, keepdims=True)
                e = jnp.exp(s - top)
                norm = jnp.sum(e, axis=0, keepdims=True)
                p = (e * (1.0 / norm)).astype(BF)
                part = dot(vt_c, p, 1, 0)
                total = part if total is None else total + part
                lse = top + jnp.log(norm)
                lse_ref[j, c : c + 1, blk] = lse[:, :128]
                lse_ref[j, 2 + c : 3 + c, blk] = lse[:, 128:]
            outs.append(total)
        a = jnp.concatenate([t[:, :128] for t in outs], axis=1).T.astype(BF)
        b = jnp.concatenate([t[:, 128:] for t in outs], axis=1).T.astype(BF)
        o_ref[:, qs] = jnp.concatenate([a, b], axis=1)

    r1 = x_ref[...].astype(F32) + dot(o_ref[...], w_ref[:, 2048:3072], 1, 1)
    r1_ref[...] = r1
    h2 = (r1 * rms_scale(r1) * gains[17:18]).astype(BF)
    h2_ref[:rows] = h2
    logits = dot(h2, w_ref[:, 3072:3200], 1, 0).T[:EXPERTS]
    at = lax.broadcasted_iota(jnp.int32, (EXPERTS, rows), 0)
    chosen = at < 0
    for t in range(routes_ref.shape[0]):
        chosen = chosen | (at == routes_ref[t : t + 1])
    logits = jnp.where(chosen, logits, neg_large)
    ex = jnp.where(chosen, jnp.exp(logits - jnp.max(logits, axis=0, keepdims=True)), 0.0)
    gates = ex / jnp.sum(ex, axis=0, keepdims=True)
    high = gates.astype(BF)
    low = (gates - high.astype(F32)).astype(BF)
    h2_ref[rows:] = jnp.concatenate([high, low], axis=1)
    keep.wait()

def forward_call(me, x, routes, seg_col, seg_row, cos, sin, pieces, spots):
    rows, width = x.shape
    s = jax.ShapeDtypeStruct
    vmem, anywhere = pl.BlockSpec(memory_space=pltpu.VMEM), pl.BlockSpec(memory_space=pl.ANY)
    return pl.pallas_call(
        functools.partial(forward_kernel, spots),
        in_specs=[pl.BlockSpec(memory_space=pltpu.SMEM)] + [vmem] * 6 + [anywhere] * len(pieces),
        out_specs=[vmem] * 8 + [anywhere],
        out_shape=[
            s((rows, width), BF),
            s((rows, 1024), BF),
            s((rows, 512), BF),
            s((rows, 512), BF),
            s((rows, 1024), BF),
            s((4, 4, rows), F32),
            s((rows, width), F32),
            s((rows + EXPERTS, width), BF),
            s((width, 3200), BF),
        ],
        scratch_shapes=[
            pltpu.VMEM((rows // BLOCK, BLOCK + MOST_DOC, BLOCK), F32),
            pltpu.VMEM((width, 3200), BF),
            pltpu.SemaphoreType.DMA((piece_count(spots),)),
            pltpu.SemaphoreType.DMA,
        ],
        cost_estimate=SMALL,
        compiler_params=pltpu.CompilerParams(vmem_limit_bytes=VMEM_ROOM),
    )(me, x, routes, seg_col, seg_row, cos, sin, *pieces)


def backward_kernel(
    spots, me_ref, p0, p1, p2, p3, p4_top, p4_low, x_ref, r1_ref, cot_ref, h1_ref, h2_ref, w_ref, q_ref, k_ref, v_ref, o_ref,
    lse_ref, seg_col_ref, seg_row_ref, cos_ref, sin_ref, ig_ref, *refs
):
    pieces, refs = refs[: len(spots)], refs[len(spots) :]
    mask_ref, do_ref, dqkv_ref, dr1_ref, wg_ref, sems = refs
    rows, width = x_ref.shape
    misc = w_ref[:, 3072:3200]
    gains = misc.astype(F32).T

    def up(ref, sl):
        return ref[sl].astype(F32)

    top, tail = slice(0, rows), slice(rows, rows + EXPERTS)
    dh2 = up(p0, top) + up(p1, top) + up(p2, top) + up(p3, top)
    half = p4_top.shape[0]
    dh2 = dh2 + jnp.concatenate([p4_top[...].astype(F32), up(p4_low, slice(0, rows - half))], axis=0)
    dg = up(p0, tail) + up(p1, tail) + up(p2, tail) + up(p3, tail) + up(p4_low, slice(rows - half, None))
    dg = dg[:, :rows] + dg[:, rows:]
    gates = up(h2_ref, tail)
    gates = gates[:, :rows] + gates[:, rows:]
    h2 = h2_ref[:rows]
    dlog = gates * (dg - jnp.sum(gates * dg, axis=0, keepdims=True))
    dlog = jnp.concatenate([dlog, jnp.zeros((128 - EXPERTS, rows), F32)], axis=0).T.astype(BF)
    dh2 = dh2 + dot(dlog, misc, 1, 1)
    r1 = r1_ref[...]
    s2 = rms_scale(r1)
    w2 = dh2 * gains[17:18]
    gain2_grad = jnp.sum(dh2 * r1 * s2, axis=0, keepdims=True)
    dr1 = cot_ref[...].astype(F32) + s2 * w2 - r1 * (s2 * s2 * s2) * jnp.mean(w2 * r1, axis=-1, keepdims=True)
    dr1_ref[...] = dr1
    dz = dr1.astype(BF)
    wg_ref[:, 2048:3072] = dot(dz, o_ref[...], 0, 0).astype(BF)
    do_ref[...] = dot(dz, w_ref[:, 2048:3072], 1, 0).astype(BF)
    router_t = dot(dlog, h2, 0, 0)
    fill_mask(mask_ref, seg_col_ref, seg_row_ref, rows)

    @pl.loop(0, 4)
    def _(j):
        qs = pl.ds(pl.multiple_of(j * 256, 256), 256)
        ks = pl.ds(pl.multiple_of(j * 128, 128), 128)
        vs = pl.ds(pl.multiple_of(1536 + j * 128, 128), 128)
        kw = pl.ds(pl.multiple_of(1024 + j * 128, 128), 128)
        cos, sin = cos_ref[...], sin_ref[...]
        def back(g):
            return (g * cos - swap_halves(g) * sin).astype(BF)
        q, k, v, do = q_ref[:, qs], k_ref[:, ks], v_ref[:, ks], do_ref[:, qs]
        kt = k.astype(F32).T.astype(BF)
        lane = lax.broadcasted_iota(jnp.int32, (rows, 128), 1)
        sub = lax.broadcasted_iota(jnp.int32, (128, rows), 0)
        dks = [jnp.zeros((BLOCK, 128), F32) for _ in range(rows // BLOCK)]
        dvs = [jnp.zeros((BLOCK, 128), F32) for _ in range(rows // BLOCK)]
        dqs = []
        for qb in range(rows // BLOCK):
            low, high = key_range(rows, qb)
            blk = slice(qb * BLOCK, (qb + 1) * BLOCK)
            q_pair = jnp.concatenate([q[blk, :128], q[blk, 128:]], axis=0)
            do_pair = jnp.concatenate([do[blk, :128], do[blk, 128:]], axis=0)
            dq_t = None
            for c in range(2):
                mine = lane[low:high] // 64 == c
                k_c = jnp.where(mine, k[low:high], BF(0))
                v_c = jnp.where(mine, v[low:high], BF(0))
                kt_c = jnp.where(sub[:, low:high] // 64 == c, kt[:, low:high], BF(0))
                s = masked_scores(mask_ref, k_c, q_pair, qb, high - low)
                lse = jnp.concatenate([lse_ref[j, c : c + 1, blk], lse_ref[j, 2 + c : 3 + c, blk]], axis=1)
                p = jnp.exp(s - lse)
                dp = dot(v_c, do_pair, 1, 1)
                inner = jnp.sum(p * dp, axis=0, keepdims=True)
                ds = (p * (dp - inner)).astype(BF)
                dk = dot(ds, q_pair, 1, 0)
                dv = dot(p.astype(BF), do_pair, 1, 0)
                t = dot(kt_c, ds, 1, 0)
                dq_t = t if dq_t is None else dq_t + t
                for i, kb in enumerate(range(low // BLOCK, high // BLOCK)):
                    sl = slice(i * BLOCK, (i + 1) * BLOCK)
                    dks[kb] = dks[kb] + jnp.where(mine[sl], dk[sl], 0.0)
                    dvs[kb] = dvs[kb] + jnp.where(mine[sl], dv[sl], 0.0)
            dqs.append(dq_t)
        dqa = jnp.concatenate([t[:, :128] for t in dqs], axis=1).T * 0.125
        dqb = jnp.concatenate([t[:, 128:] for t in dqs], axis=1).T * 0.125
        dqkv_ref[:, qs] = jnp.concatenate([back(dqa), back(dqb)], axis=1)
        dqkv_ref[:, kw] = back(jnp.concatenate(dks, axis=0))
        dqkv_ref[:, vs] = jnp.concatenate(dvs, axis=0).astype(BF)

    dqkv = dqkv_ref[...]
    wg_ref[:, :2048] = dot(h1_ref[...], dqkv, 0, 0).astype(BF)
    dh1 = dot(dqkv, w_ref[:, :2048], 1, 1)
    x = x_ref[...].astype(F32)
    s1 = rms_scale(x)
    w1 = dh1 * gains[16:17]
    gain1_grad = jnp.sum(dh1 * x * s1, axis=0, keepdims=True)
    ig_ref[...] = dr1_ref[...] + s1 * w1 - x * (s1 * s1 * s1) * jnp.mean(w1 * x, axis=-1, keepdims=True)
    at = lax.broadcasted_iota(jnp.int32, (128, width), 0)
    misc_t = jnp.where(at == 16, gain1_grad, jnp.where(at == 17, gain2_grad, router_t))
    wg_ref[:, 3072:3200] = misc_t.T.astype(BF)
    copies = piece_copies(me_ref, spots, pieces, wg_ref, sems, False)
    for copy in copies:
        copy.start()
    for copy in copies:
        copy.wait()

def backward_call(me, parts, x, r1, cot, h1, h2, w, q, k, v, o, lse, seg_col, seg_row, cos, sin, piece_shapes, spots):
    rows, width = x.shape
    s = jax.ShapeDtypeStruct
    vmem, anywhere = pl.BlockSpec(memory_space=pltpu.VMEM), pl.BlockSpec(memory_space=pl.ANY)
    return pl.pallas_call(
        functools.partial(backward_kernel, spots),
        in_specs=[pl.BlockSpec(memory_space=pltpu.SMEM)] + [vmem] * 21,
        out_specs=[vmem] + [anywhere] * len(spots),
        out_shape=[s((rows, width), F32)] + [s(shape, BF) for shape in piece_shapes],
        scratch_shapes=[
            pltpu.VMEM((rows // BLOCK, BLOCK + MOST_DOC, BLOCK), F32),
            pltpu.VMEM((rows, 1024), BF),
            pltpu.VMEM((rows, 2048), BF),
            pltpu.VMEM((rows, width), F32),
            pltpu.VMEM((width, 3200), BF),
            pltpu.SemaphoreType.DMA((piece_count(spots),)),
        ],
        cost_estimate=SMALL,
        compiler_params=pltpu.CompilerParams(vmem_limit_bytes=VMEM_ROOM),
    )(me, *parts, x, r1, cot, h1, h2, w, q, k, v, o, lse, seg_col, seg_row, cos, sin)


def expert_kernel(plan, count, place_ref, *refs):
    arrays, refs = refs[:count], refs[count:]
    w_refs = refs[:6]
    ug0, ug1, da0, da1, db0, db1, dg_ref, h_all, g_all, h_buf, g_buf, sems = refs[-12:]
    rows = g_buf.shape[1]
    step = pl.program_id(0)

    def copies(i):
        found = []
        for buf, parts in ((h_buf, plan[i][0]), (g_buf, plan[i][1])):
            for array, start, size, at in parts:
                sem = sems.at[i % 2, len(found)]
                found.append(
                    pltpu.make_async_copy(
                        arrays[array].at[pl.ds(start, size)], buf.at[i % 2, pl.ds(at, size)], sem
                    )
                )
        return found

    for i in range(len(plan)):

        @pl.when(step == i)
        def _(i=i):
            if i == 0:
                for copy in copies(0):
                    copy.start()
            if i + 1 < len(plan):
                for copy in copies(i + 1):
                    copy.start()
            for copy in copies(i):
                copy.wait()

    slot = lax.rem(step, 2)
    h = h_buf[slot, :rows]
    g = g_buf[slot]
    tail = h_buf[slot, rows:].astype(F32)
    tail = tail[:, :rows] + tail[:, rows:]
    gates = jnp.concatenate([tail, jnp.zeros((128 - EXPERTS, rows), F32)], axis=0).T
    h_all[...] = h
    g_all[...] = g
    lane = lax.broadcasted_iota(jnp.int32, (rows, 128), 1)
    totals = []
    for e, (ug_ref, da_ref, db_ref) in enumerate(((ug0, da0, db0), (ug1, da1, db1))):
        wg_ref, wu_ref, wd_ref = w_refs[3 * e : 3 * e + 3]
        ff = wg_ref.shape[2]
        gate = jnp.sum(jnp.where(lane == place_ref[0] * MINE + e, gates, 0.0), axis=1, keepdims=True)
        total = 0.0
        for half in range(2):
            sl = slice(half * ff // 2, (half + 1) * ff // 2)
            a = dot(h, wg_ref[0, :, sl], 1, 0)
            b = dot(h, wu_ref[0, :, sl], 1, 0)
            gd = dot(g, wd_ref[0, :, sl], 1, 0)
            sigma = 1.0 / (1.0 + jnp.exp(-a))
            silu = a * sigma
            u = (silu * b).astype(BF).astype(F32)
            total = total + jnp.sum(u * gd, axis=1, keepdims=True)
            ug_ref[:, sl] = (u * gate).astype(BF)
            du = gd * gate
            db_ref[:, sl] = (du * silu).astype(BF)
            da_ref[:, sl] = (du * b * (sigma * (1.0 + a * (1.0 - sigma)))).astype(BF)
        totals.append(total)
    dg_ref[0] = jnp.where(lane == 0, totals[0], totals[1]).T[:8]


def expert_call(place, arrays, plan, weights, first, kept):
    _, width, ff = weights.shape
    rows = sum(piece[2] for piece in plan[0][1])
    most = max(len(h) + len(g) for h, g in plan)
    s = jax.ShapeDtypeStruct
    at = lambda i: (first + i, 0)
    anywhere = pl.BlockSpec(memory_space=pl.ANY)
    tile, hidden = pl.BlockSpec((rows, width), at), pl.BlockSpec((rows, ff), at)
    held = 1 + len(arrays) + 6
    return pl.pallas_call(
        functools.partial(expert_kernel, plan, len(arrays)),
        grid=(len(plan),),
        in_specs=[pl.BlockSpec(memory_space=pltpu.SMEM)]
        + [anywhere] * len(arrays)
        + [pl.BlockSpec((1, width, ff), lambda i, k=k: (k, 0, 0), pipeline_mode=pl.Buffered(1)) for k in range(6)]
        + [anywhere] * len(kept),
        out_specs=[hidden] * 6 + [pl.BlockSpec((1, 8, rows), lambda i: (first + i, 0, 0))] + [tile] * 2,
        out_shape=[s((PLANE * rows, ff), BF)] * 6
        + [s((PLANE, 8, rows), F32)]
        + [s((PLANE * rows, width), BF)] * 2,
        input_output_aliases={held + i: i for i in range(len(kept))},
        scratch_shapes=[
            pltpu.VMEM((2, rows + EXPERTS, width), BF),
            pltpu.VMEM((2, rows, width), BF),
            pltpu.SemaphoreType.DMA((2, most)),
        ],
        cost_estimate=SMALL,
        compiler_params=pltpu.CompilerParams(vmem_limit_bytes=VMEM_ROOM),
    )(place, *arrays, *[weights] * 6, *kept)


def turn_back_kernel(pairs, count, tailed, *refs):
    refs = list(refs)
    if tailed:
        place_ref, dg_ref = refs[:2]
        refs = refs[2:]
    outs, buf, sems = refs[2 * pairs : 2 * pairs + count], refs[-2], refs[-1]
    step = pl.program_id(0)
    slot = lax.rem(step, 2)

    def copy(i):
        return pltpu.make_async_copy(buf.at[i % 2], outs[i], sems.at[i % 2])

    for i in range(2, count):

        @pl.when(step == i)
        def _(i=i):
            copy(i - 2).wait()

    total = 0.0
    for i in range(pairs):
        total = total + dot(refs[i][...], refs[pairs + i][0], 1, 1)
    rows = total.shape[0]
    buf[slot, :rows] = total.astype(BF)
    if tailed:
        place = place_ref[0]
        at = lax.broadcasted_iota(jnp.int32, (EXPERTS, rows), 0)
        dg = jnp.where(
            at == place * MINE, dg_ref[0, :1], jnp.where(at == place * MINE + 1, dg_ref[0, 1:2], 0.0)
        )
        high = dg.astype(BF)
        low = (dg - high.astype(F32)).astype(BF)
        buf[slot, rows:] = jnp.concatenate([high, low], axis=1)
    for i in range(count):

        @pl.when(step == i)
        def _(i=i):
            copy(i).start()
            if i == count - 1:
                copy(i - 1).wait()
                copy(i).wait()


def turn_back(first, count, acts, weights, kinds, tail):
    rows = acts[0].shape[0] // PLANE
    _, width, ff = weights.shape
    extra = EXPERTS if tail else 0
    in_specs, operands = [], []
    if tail:
        in_specs = [
            pl.BlockSpec(memory_space=pltpu.SMEM),
            pl.BlockSpec((1, 8, rows), lambda i: (first + i, 0, 0)),
        ]
        operands = list(tail)
    in_specs += [pl.BlockSpec((rows, ff), lambda i: (first + i, 0))] * len(acts)
    in_specs += [
        pl.BlockSpec((1, width, ff), lambda i, k=k: (k, 0, 0), pipeline_mode=pl.Buffered(1)) for k in kinds
    ]
    return pl.pallas_call(
        functools.partial(turn_back_kernel, len(acts), count, bool(tail)),
        grid=(count,),
        in_specs=in_specs,
        out_specs=[pl.BlockSpec(memory_space=pl.ANY)] * count,
        out_shape=[jax.ShapeDtypeStruct((rows + extra, width), BF)] * count,
        scratch_shapes=[pltpu.VMEM((2, rows + extra, width), BF), pltpu.SemaphoreType.DMA((2,))],
        cost_estimate=SMALL,
        compiler_params=pltpu.CompilerParams(vmem_limit_bytes=VMEM_ROOM),
    )(*operands, *acts, *[weights] * len(kinds))


def weight_grad_kernel(count, left_ref, *refs):
    rights, out_ref, acc_ref = refs[:count], refs[count], refs[count + 1]
    k = pl.program_id(0)
    ff = rights[0].shape[1]
    part = dot(left_ref[...], jnp.concatenate([r[...] for r in rights], axis=1), 0, 0)

    @pl.when(k == 0)
    def _():
        acc_ref[...] = part

    @pl.when(k > 0)
    def _():
        acc_ref[...] += part

    @pl.when(k == pl.num_programs(0) - 1)
    def _():
        for t in range(count):
            out_ref[t] = acc_ref[:, t * ff : (t + 1) * ff].astype(BF)


def weight_grads(left, rights):
    total, width = left.shape
    ff = rights[0].shape[1]
    count = len(rights)
    step = total // 4
    row = lambda i: (i, 0)
    return pl.pallas_call(
        functools.partial(weight_grad_kernel, count),
        grid=(4,),
        in_specs=[pl.BlockSpec((step, width), row)] + [pl.BlockSpec((step, ff), row)] * count,
        out_specs=pl.BlockSpec((count, width, ff), lambda i: (0, 0, 0), pipeline_mode=pl.Buffered(1)),
        out_shape=jax.ShapeDtypeStruct((count, width, ff), BF),
        scratch_shapes=[pltpu.VMEM((width, count * ff), F32)],
        cost_estimate=SMALL,
        compiler_params=pltpu.CompilerParams(vmem_limit_bytes=VMEM_ROOM),
    )(left, *rights)


def up(v):
    return v.astype(F32)


def after(value, *others):
    return lax.optimization_barrier((value, *others))[0]


CUT = 1536
COLUMNS = 3200


def make_local(n):
    outer = n // PLANE
    plane_groups = [[PLANE * z + i for i in range(PLANE)] for z in range(outer)]
    outer_groups = [[PLANE * z + i for z in range(outer)] for i in range(PLANE)]
    pieced = outer == 4

    def swap(array, offset):
        return lax.ppermute(array, "dp", [(i, i ^ offset) for i in range(n)])

    along_z = [PLANE * k for k in range(4)]

    def dense_gather(part, *earlier):
        if not pieced:
            return [lax.all_gather(part, "dp", axis=0, tiled=True)], [(None, 0)]
        line = after([part] + [swap(part, k) for k in along_z[1:]], *earlier)
        left, right = jnp.stack([t[:, :CUT] for t in line]), jnp.stack([t[:, CUT:] for t in line])
        left_x, right_y = swap(left, 2), swap(right, 4)
        left_y, right_x = swap(left, 4), swap(right, 2)
        left_xy, right_xy = swap(left_x, 4), swap(right_y, 2)
        found = [(left, 0, 0), (left_x, 2, 0), (left_y, 4, 0), (left_xy, 6, 0)]
        found += [(right, 0, CUT), (right_x, 2, CUT), (right_y, 4, CUT), (right_xy, 6, CUT)]
        found += [(swap(piece, 1), offset + 1, first) for piece, offset, first in found]
        return [f[0] for f in found], [([f[1] + k for k in along_z], f[2]) for f in found]

    def grad_spots(share):
        if not pieced:
            return [(n * share, COLUMNS)], [(None, 0)]
        shapes, spots = [], []
        for core in (1, 0):
            for major, minor, first, cols in ((2, 4, 0, CUT), (4, 2, CUT, COLUMNS - CUT)):
                for far in (0, major):
                    shapes.append((8, share, cols))
                    spots.append(([core + far + d + k for d in (0, minor) for k in along_z], first))
        return shapes, spots

    def dense_sum(pieces):
        if not pieced:
            return up(lax.psum_scatter(pieces[0], "dp", scatter_dimension=0, tiled=True)), (pieces[0],)

        def add(a, b):
            return (up(a) + up(b)).astype(BF)

        near_l, far_l, near_r, far_r = (add(keep, swap(sent, 1)) for sent, keep in zip(pieces[:4], pieces[4:]))
        got_l, got_r = swap(far_l, 2), swap(far_r, 4)
        sent_l, sent_r = add(near_l[4:], got_l[4:]), add(near_r[4:], got_r[4:])
        left = add(add(near_l[:4], got_l[:4]), swap(sent_l, 4))
        right = add(add(near_r[:4], got_r[:4]), swap(sent_r, 2))
        both = jnp.concatenate([left, right], axis=2)
        total = up(both[0])
        for k in range(1, 4):
            total = total + up(swap(both[k], PLANE * k))
        return total, (both,)

    def both_cores(same_core):
        return [b for part in same_core for b in (part, swap(part, 1))]

    def local(
        tokens,
        query_weight,
        key_projection_weight,
        value_projection_weight,
        output_weight,
        first_gain,
        second_gain,
        router_weight,
        gate_weight,
        up_weight,
        down_weight,
        routes,
        segments,
        cotangent,
    ):
        rows, width = tokens.shape
        ff = gate_weight.shape[2]
        share = query_weight.shape[0]
        me = lax.axis_index("dp").astype(jnp.int32).reshape(1)
        place = lax.rem(me, PLANE)

        def paired(w):
            return w.reshape(-1, 4, 2, 2, HEAD_SIZE).swapaxes(2, 3).reshape(-1, HEADS * HEAD_SIZE)

        expert_part = jnp.stack(
            [w.reshape(PLANE, MINE, share, ff) for w in (gate_weight, up_weight, down_weight.transpose(0, 2, 1))],
            axis=2,
        )
        dense_part = jnp.concatenate(
            [
                paired(query_weight),
                key_projection_weight,
                value_projection_weight,
                paired(output_weight.T),
                router_weight,
                first_gain[:, None],
                second_gain[:, None],
                jnp.zeros((share, 128 - EXPERTS - 2), BF),
            ],
            axis=1,
        )
        dense_part = after(dense_part, expert_part)
        expert_part = lax.all_to_all(
            expert_part, "dp", split_axis=0, concat_axis=0, axis_index_groups=plane_groups
        )

        expert_part = expert_part.transpose(1, 2, 0, 3, 4).reshape(3 * MINE, PLANE * share, ff)
        weights = lax.all_gather(expert_part, "dp", axis=1, tiled=True, axis_index_groups=outer_groups)

        positions = jnp.arange(rows, dtype=F32)
        frequency = 10000.0 ** (-2.0 * jnp.arange(HEAD_SIZE // 2, dtype=F32) / HEAD_SIZE)
        angles = positions[:, None] * frequency[None, :]
        cosine, sine = jnp.cos(angles), jnp.sin(angles)
        cosine = jnp.concatenate([cosine] * 4, axis=1)
        sine = jnp.concatenate([-sine, sine, -sine, sine], axis=1)
        seg_col = segments.reshape(rows, 1)
        seg_row = segments.reshape(1, rows)

        half = rows // 2
        pieces, spots = dense_gather(dense_part, cosine, sine, seg_col)
        late = after(cotangent, *pieces)
        cot_x, cot_y = swap(late, 2), swap(late, 4)

        h1, q, k, v, o, lse, r1, h2, dense = forward_call(
            me, tokens, routes.T, seg_col, seg_row, cosine, sine, pieces, spots
        )
        h2 = after(h2, cot_x, cot_y)
        h2_x, h2_y, h2_core = swap(h2, 2), swap(h2, 4), swap(h2, 1)
        cot_core = swap(cotangent, 1)
        h2_x, h2_y, cot_x, cot_y = after((h2_x, h2_y, cot_x, cot_y), h2_core, cot_core)
        corner_x = swap(jnp.concatenate([h2_y[:half], cot_y[:half]], axis=0), 2)
        corner_y = swap(jnp.concatenate([h2_x[half:], cot_x[half:]], axis=0), 4)
        cores = [swap(t, 1) for t in (h2_x, cot_x, h2_y, cot_y)]
        long = rows + EXPERTS

        def pieces_of(h, g):
            return ([(h, 0, long, 0)], [(g, 0, rows, 0)])

        near_arrays = [h2, h2_core, h2_x, cores[0], cotangent, cot_core, cot_x, cores[1]]
        near_plan = [pieces_of(i, 4 + i) for i in range(4)]
        kept = expert_call(after(place, *cores), near_arrays, near_plan, weights, 0, ())
        corner_x, corner_y = after((corner_x, corner_y), *cores)
        far_arrays = [h2_y, cores[2], cot_y, cores[3], corner_x, swap(corner_x, 1), corner_y, swap(corner_y, 1)]
        far_plan = [pieces_of(i, 2 + i) for i in range(2)]
        far_plan += [
            (
                [(i, 0, half, 0), (i + 2, 0, long - half, half)],
                [(i, half, half, 0), (i + 2, long - half, half, half)],
            )
            for i in (4, 5)
        ]
        kept = expert_call(place, far_arrays, far_plan, weights, 4, kept)
        ug0, ug1, da0, da1, db0, db1, dg, tokens_all, grads_all = kept

        def outer_sum(grads):
            return lax.psum_scatter(grads, "dp", scatter_dimension=1, tiled=True, axis_index_groups=outer_groups)

        back = functools.partial(turn_back, acts=[da0, db0, da1, db1], weights=weights, kinds=[0, 1, 3, 4])

        def with_core(block, other):
            return (up(block) + up(other)).astype(BF)

        top, low = slice(0, half), slice(half, None)

        def together(*values):
            return lax.optimization_barrier(values)

        far = back(4, 4, tail=(place, dg))
        place, far = together(place, far)

        near, far_core = back(0, 4, tail=(place, dg)), (swap(far[1], 1), swap(far[3], 1))
        near, far, far_core = together(near, far, far_core)
        sum_y = with_core(far[0], far_core[0])
        sum_xy = [with_core(far[2][part], far_core[1][part]) for part in (top, low)]
        sum_y, sum_xy, near, grads_all = together(sum_y, sum_xy, near, grads_all)

        grads_d, got_top = weight_grads(grads_all, [ug0, ug1]), swap(sum_xy[0], 6)
        near_core = swap(near[1], 1), swap(near[3], 1)
        grads_d, got_top, near_core, near, sum_xy, sum_y = together(grads_d, got_top, near_core, near, sum_xy, sum_y)
        sums_d = outer_sum(grads_d)
        sum_x = with_core(near[2], near_core[1])
        sum_x, sum_xy, ug0 = together(sum_x, sum_xy, ug0)

        out, got_low = turn_back(0, PLANE, [ug0, ug1], weights, [2, 5], None), swap(sum_xy[1], 6)
        out, got_low, sum_x, sum_y, tokens_all = together(out, got_low, sum_x, sum_y, tokens_all)

        grads_gu, got_x, got_y = weight_grads(tokens_all, [da0, da1, db0, db1]), swap(sum_x, 2), swap(sum_y, 4)
        out_core = [swap(out[i], 1) for i in (1, 3, 5, 7)]
        grads_gu, got_x, got_y, out, out_core = together(grads_gu, got_x, got_y, out, out_core)
        sums_gu = outer_sum(grads_gu)
        out_x, out_y = with_core(out[2], out_core[1]), with_core(out[4], out_core[2])
        out_xy = [with_core(out[6][part], out_core[3][part]) for part in (top, low)]
        got = [near[0], near_core[0], got_x, got_y, got_top, got_low]
        got, out_x, out_y, out_xy = together(got, out_x, out_y, out_xy)

        shapes, grad_places = grad_spots(share)
        input_grad, *grad_pieces = backward_call(
            me, got, tokens, r1, cotangent, h1, h2, dense, q, k, v, o, lse, seg_col, seg_row, cosine, sine,
            shapes, grad_places,
        )
        out_got = swap(out_x, 2), swap(out_y, 4), swap(out_xy[0], 6)
        input_grad, grad_pieces, out_got, out_xy = together(input_grad, grad_pieces, out_got, out_xy)

        dense_grads, moment = dense_sum(grad_pieces)
        out_low = swap(after(out_xy[1], *moment), 6)
        output = r1 + up(out[0]) + up(out_core[0]) + up(out_got[0]) + up(out_got[1])
        output = (output + jnp.concatenate([up(out_got[2]), up(out_low)], axis=0)).astype(BF)

        def to_owner(grads):
            grads = grads.reshape(-1, PLANE, share, ff).transpose(1, 0, 2, 3)
            return lax.all_to_all(grads, "dp", split_axis=0, concat_axis=0, axis_index_groups=plane_groups)

        owned_d = to_owner(after(sums_d, *moment))
        owned_gu = to_owner(after(sums_gu, owned_d))

        def experts_of(first, second):
            return up(jnp.stack([first, second], axis=1)).reshape(EXPERTS, share, ff)

        gate_out = experts_of(owned_gu[:, 0], owned_gu[:, 1])
        up_out = experts_of(owned_gu[:, 2], owned_gu[:, 3])
        down_out = experts_of(owned_d[:, 0], owned_d[:, 1]).transpose(0, 2, 1)

        return (
            output,
            input_grad,
            paired(dense_grads[:, :1024]),
            dense_grads[:, 1024:1536],
            dense_grads[:, 1536:2048],
            paired(dense_grads[:, 2048:3072]).T,
            dense_grads[:, 3072 + EXPERTS],
            dense_grads[:, 3073 + EXPERTS],
            dense_grads[:, 3072 : 3072 + EXPERTS],
            gate_out,
            up_out,
            down_out,
        )

    return local


def solution(mesh):
    row, col, one = P("dp", None), P(None, "dp"), P("dp")
    middle, last = P(None, "dp", None), P(None, None, "dp")
    in_specs = (row, row, row, row, col, one, one, row, middle, middle, last, row, row, row)
    out_specs = (row, row, row, row, row, col, one, one, row, middle, middle, last)
    return jax.shard_map(
        make_local(mesh.shape["dp"]), mesh=mesh, in_specs=in_specs, out_specs=out_specs, check_vma=False
    )
```

time: 748 us -> 443 us (0.59)
  matrix products: 222 us -> 0 us
  Pallas kernels: 0 us -> 184 us
  waiting for transfers between devices: 277 us -> 133 us
  local copies, waits for them, and re-layouts: 94.8 us -> 18.8 us
  other arithmetic: 90.1 us -> 28.7 us
  starting transfers between devices: 39.8 us -> 59 us
    dot_general x26 -> x0, matrix products: 222 us -> none  [the longest x20 179 us: dot(): lax.dot_general(a, b, (((ca,), (cb,)), ((), ())), preferred_element_type=...]
    pallas_call x0 -> x9, Pallas kernels: none -> 184 us  [the longest x2 45 us: expert_call(): pl.pallas_call(functools.partial(expert_kernel, plan, len(arrays)), grid=...]
    reduce_scatter x2, waiting for transfers between devices: 90.2 us -> 0.01 us  [outer_sum(): lax.psum_scatter(grads, 'dp', scatter_dimension=1, tiled=True, axis_index...]
    all_gather x2 -> x1, waiting for transfers between devices: 31.5 us -> 0.01 us  [local(): lax.all_gather(expert_part, 'dp', axis=1, tiled=True, axis_index_groups=o...]
    unnamed x143 -> x114, local copies, waits for them, and re-layouts: 37.3 us -> 7.01 us
    all_to_all x1 -> x2, waiting for transfers between devices: 32.9 us -> 7.4 us  [to_owner(): lax.all_to_all(grads, 'dp', split_axis=0, concat_axis=0, axis_index_group...]
    convert_element_type x15 -> x16, other arithmetic: 41 us -> 18.9 us  [the longest x7 12.2 us: with_core(): return (up(block) + up(other)).astype(BF)]
    concatenate x14 -> x3, other arithmetic: 20.9 us -> 1.43 us  [the longest x1 1.29 us: local(): cosine = jnp.concatenate([cosine] * 4, axis=1)]
  transfers between devices with their start and end apart: 38 -> 64, of which waited for: 14 -> 25; matrix products, arithmetic and copies ran while one was open for 34% -> 7% of each run, Pallas kernels for 0% -> 34%
where the time goes in v2:
time: 443 us; the launch traced here: 440 us
  Pallas kernels  184 us (42%)
  waiting for transfers between devices  133 us (30%)
  starting transfers between devices  59 us (13%)
  other arithmetic  28.7 us (6%)
  local copies, waits for them, and re-layouts  18.8 us (4%)
  between operations  15.2 us (3%)
    ppermute x58, waiting for transfers between devices, swap(): return lax.ppermute(array, 'dp', [(i, i ^ offset) for i in range(n)])  126 us
    ppermute x58, starting transfers between devices, swap(): return lax.ppermute(array, 'dp', [(i, i ^ offset) for i in range(n)])  46 us
    pallas_call x2, Pallas kernels, expert_call(): pl.pallas_call(functools.partial(expert_kernel, plan, len(arrays)), grid=...  45 us
    pallas_call x3, Pallas kernels, turn_back(): pl.pallas_call(functools.partial(turn_back_kernel, len(acts), count, bool...  42 us
    pallas_call x2, Pallas kernels, weight_grads(): pl.pallas_call(functools.partial(weight_grad_kernel, count), grid=(4,), i...  41.2 us
    pallas_call x1, Pallas kernels, backward_call(): pl.pallas_call(functools.partial(backward_kernel, spots), in_specs=[pl.Bl...  34.4 us
    pallas_call x1, Pallas kernels, forward_call(): pl.pallas_call(functools.partial(forward_kernel, spots), in_specs=[pl.Blo...  21.8 us
    convert_element_type x7, other arithmetic, with_core(): return (up(block) + up(other)).astype(BF)  12.2 us
  transfers between devices with their start and end apart: 64, of which 25 were waited for; matrix products, arithmetic and copies ran while one was open for 7% of the time, Pallas kernels for 34%

profile of v2, /device:TPU:0, one launch (start us, length us, event | category | flops | bytes accessed | tf_op | source)
XLA Modules:
  0.0 439.7 jit_solution(6576163706951396672)
XLA Ops:
  7.2 2.7 pad_maximum_fusion
  9.9 5.3 %all-to-all-start = ((bf16[8,2,3,32,512]{4,3,2,1,0:T(8,128)(2,1)}), bf16[8,2,3,32,512]{4,3,2,1,0:T(8,128)(2,1)S(1)}, u32[]{:S(2)}, u32[]{:S(2)}) async-start(bf16[8,2,3,32,512]{4,3,2,1,0:T(8,128)(2,1)} %pad_maximum_fusion), calls=%async_computation | async-start | bytes 3145728 | tf_op jit(solution)/shard_map/all_to_all | solution.py:621
  16.5 3.7 collective-permute-start.2
  23.2 3.1 collective-permute-done.2
  26.4 11.8 %collective-permute-done.1 = bf16[32,3200]{1,0:T(8,128)(2,1)S(1)} collective-permute-done((bf16[32,3200]{1,0:T(8,128)(2,1)S(1)}, bf16[32,3200]{1,0:T(8,128)(2,1)S(1)}, u32[]{:S(2)}, u32[]{:S(2)}) %collective-permute-start.1) | collective-permute-done | bytes 204832 | tf_op jit(solution)/shard_map/ppermute | solution.py:529
  40.2 1.7 collective-permute-start.7
  42.5 1.7 collective-permute-start.3
  45.4 7.6 %collective-permute-done.7.refs_6_ = bf16[4,32,1664]{2,1,0:T(8,128)(2,1)S(1)} collective-permute-done((bf16[4,32,1664]{2,1,0:T(8,128)(2,1)S(1)}, bf16[4,32,1664]{2,1,0:T(8,128)(2,1)S(1)}, u32[]{:S(2)}, u32[]{:S(2)}) %collective-permute-start.7) | collective-permute-done | bytes 426016 | tf_op jit(solution)/shard_map/ppermute | solution.py:529
  52.9 1.7 collective-permute-start.8
  54.6 5.4 %collective-permute-done.4.refs_2_ = bf16[4,32,1536]{2,1,0:T(8,128)(2,1)S(1)} collective-permute-done((bf16[4,32,1536]{2,1,0:T(8,128)(2,1)S(1)}, bf16[4,32,1536]{2,1,0:T(8,128)(2,1)S(1)}, u32[]{:S(2)}, u32[]{:S(2)}) %collective-permute-start.4) | collective-permute-done | bytes 393248 | tf_op jit(solution)/shard_map/ppermute | solution.py:529
  61.6 2.0 collective-permute-done.6.refs_5_
  63.6 8.3 %collective-permute-done.8.refs_7_ = bf16[4,32,1664]{2,1,0:T(8,128)(2,1)S(1)} collective-permute-done((bf16[4,32,1664]{2,1,0:T(8,128)(2,1)S(1)}, bf16[4,32,1664]{2,1,0:T(8,128)(2,1)S(1)}, u32[]{:S(2)}, u32[]{:S(2)}) %collective-permute-start.8) | collective-permute-done | bytes 426016 | tf_op jit(solution)/shard_map/ppermute | solution.py:529
  72.6 1.7 collective-permute-done.10.refs_9_
  74.9 1.7 collective-permute-start.18
  79.1 21.8 %shard_map.229 = (bf16[512,1024]{1,0:T(8,128)(2,1)}, bf16[512,1024]{1,0:T(8,128)(2,1)}, bf16[512,512]{1,0:T(8,128)(2,1)}, bf16[512,512]{1,0:T(8,128)(2,1)}, bf16...) custom-call(s32[1]{0:T(128)} %bitcast.me_ref, ...), custom_call_target="tpu_custom_call" | custom-call | flops 1 | bytes 1 | tf_op jit(solution)/shard_map/pallas_call | solution.py:158
  102.0 1.6 collective-permute-start.19
  103.6 2.7 collective-permute-done.22.refs_5_
  106.3 21.8 %collective-permute-done.20.refs_0_ = bf16[528,1024]{1,0:T(8,128)(2,1)S(1)} collective-permute-done((bf16[528,1024]{1,0:T(8,128)(2,1)}, bf16[528,1024]{1,0:T(8,128)(2,1)S(1)}, u32[]{:S(2)}, u32[]{:S(2)}) %collective-permute-start.20) | collective-permute-done | bytes 1081376 | tf_op jit(solution)/shard_map/ppermute | solution.py:529
  128.3 1.7 collective-permute-start.25
  132.3 20.9 %collective-permute-done.25.refs_4_ = bf16[512,1024]{1,0:T(8,128)(2,1)S(1)} collective-permute-done((bf16[512,1024]{1,0:T(8,128)(2,1)S(1)}, bf16[512,1024]{1,0:T(8,128)(2,1)S(1)}, u32[]{:S(2)}, u32[]{:S(2)}) %collective-permute-start.25) | collective-permute-done | bytes 1048608 | tf_op jit(solution)/shard_map/ppermute | solution.py:529
  153.3 2.6 collective-permute-done.28.refs_7_
  157.7 22.4 %shard_map.230 = (bf16[4096,512]{1,0:T(8,128)(2,1)}, bf16[4096,512]{1,0:T(8,128)(2,1)}, bf16[4096,512]{1,0:T(8,128)(2,1)}, bf16[4096,512]{1,0:T(8,128)(2,1)}, bf...) custom-call(s32[1]{0:T(128)S(6)} %rem.18.place_ref.refs_0_, ...), custom_call_target="tpu_custom_call" | custom-call | flops 1 | bytes 1 | tf_op jit(solution)/shard_map/pallas_call | solution.py:381
  181.1 22.6 %shard_map.231 = (bf16[4096,512]{1,0:T(8,128)(2,1)}, bf16[4096,512]{1,0:T(8,128)(2,1)}, bf16[4096,512]{1,0:T(8,128)(2,1)}, bf16[4096,512]{1,0:T(8,128)(2,1)}, bf...) custom-call(s32[1]{0:T(128)S(6)} %rem.18.place_ref.refs_0_, ...), custom_call_target="tpu_custom_call", output_to_operand_aliasing={{0}: (15, {}), {1}: (16, {}), {2}: (17, {}), {3}: (18, {}),... | custom-call | flops 1 | bytes 1 | tf_op jit(solution)/shard_map/pallas_call | solution.py:381
  203.8 13.8 %shard_map.232 = (bf16[528,1024]{1,0:T(8,128)(2,1)}, bf16[528,1024]{1,0:T(8,128)(2,1)}, bf16[528,1024]{1,0:T(8,128)(2,1)}, bf16[528,1024]{1,0:T(8,128)(2,1)}) custom-call(s32[1]{0:T(128)S(6)} %rem.18.place_ref.refs_0_, f32[8,8,512]{2,1,0:T(8,128)} %get-tuple-element.184.refs_1_, bf16[4096,512]{1,0:T(8,128)(2,1)} %get-tuple-element.185.refs_2_.refs_0_, ...), custom_call_target="tpu_custom_call" | custom-call | flops 1 | bytes 1 | tf_op jit(solution)/shard_map/pallas_call | solution.py:460
  218.2 13.7 %shard_map.233 = (bf16[528,1024]{1,0:T(8,128)(2,1)}, bf16[528,1024]{1,0:T(8,128)(2,1)}, bf16[528,1024]{1,0:T(8,128)(2,1)}, bf16[528,1024]{1,0:T(8,128)(2,1)}) custom-call(s32[1]{0:T(128)S(6)} %rem.18.place_ref.refs_0_, f32[8,8,512]{2,1,0:T(8,128)} %get-tuple-element.184.refs_1_, bf16[4096,512]{1,0:T(8,128)(2,1)} %get-tuple-element.185.refs_2_.refs_0_, ...), custom_call_target="tpu_custom_call" | custom-call | flops 1 | bytes 1 | tf_op jit(solution)/shard_map/pallas_call | solution.py:460
  234.9 2.3 collective-permute-start.33
  237.2 14.7 %shard_map.234 = bf16[2,1024,512]{2,1,0:T(8,128)(2,1)} custom-call(bf16[4096,1024]{1,0:T(8,128)(2,1)} %get-tuple-element.211.left_ref, bf16[4096,512]{1,0:T(8,128)(2,1)} %get-tuple-element.224.refs_0_, bf16[4096,512]{1,0:T(8,128)(2,1)} %get-tuple-element.213.refs_1_), custom_call_target="tpu_custom_call" | custom-call | flops 1 | bytes 1 | tf_op jit(solution)/shard_map/pallas_call | solution.py:498
  253.6 2.6 add_convert_fusion
  256.9 14.5 %shard_map.235 = (bf16[512,1024]{1,0:T(8,128)(2,1)}, bf16[512,1024]{1,0:T(8,128)(2,1)}, bf16[512,1024]{1,0:T(8,128)(2,1)}, bf16[512,1024]{1,0:T(8,128)(2,1)}, bf...) custom-call(bf16[4096,512]{1,0:T(8,128)(2,1)} %get-tuple-element.224, ...), custom_call_target="tpu_custom_call" | custom-call | flops 1 | bytes 1 | tf_op jit(solution)/shard_map/pallas_call | solution.py:460
  275.1 26.5 %shard_map.236 = bf16[4,1024,512]{2,1,0:T(8,128)(2,1)} custom-call(bf16[4096,1024]{1,0:T(8,128)(2,1)} %get-tuple-element.237.left_ref, bf16[4096,512]{1,0:T(8,128)(2,1)} %get-tuple-element.185.refs_2_.refs_0_, bf16[4096,512]{1,0:T(8,128)(2,1)} %get-tuple-element.187.refs_4_.refs_1_, bf16[4096,512]{1,0:T(8,128)(2,1)} %get-tuple-element.186.refs_3_.refs_2_, ...), custom_call_target="tpu_custom_call" | custom-call | flops 1 | bytes 1 | tf_op jit(solution)/shard_map/pallas_call | solution.py:498
  303.7 2.7 add_convert_fusion.4
  306.3 1.9 add_convert_fusion.3
  308.3 2.6 add_convert_fusion.10
  314.4 34.4 %shard_map.237 = (f32[512,1024]{1,0:T(8,128)}, bf16[8,32,1536]{2,1,0:T(8,128)(2,1)}, bf16[8,32,1536]{2,1,0:T(8,128)(2,1)}, bf16[8,32,1664]{2,1,0:T(8,128)(2,1)},...) custom-call(s32[1]{0:T(128)} %bitcast.me_ref, ...), custom_call_target="tpu_custom_call" | custom-call | flops 1 | bytes 1 | tf_op jit(solution)/shard_map/pallas_call | solution.py:290
  356.4 15.9 %collective-permute-done.48 = bf16[8,32,1536]{2,1,0:T(8,128)(2,1)S(1)} collective-permute-done((bf16[8,32,1536]{2,1,0:T(8,128)(2,1)S(1)}, bf16[8,32,1536]{2,1,0:T(8,128)(2,1)S(1)}, u32[]{:S(2)}, u32[]{:S(2)}) %collective-permute-start.48) | collective-permute-done | bytes 786464 | tf_op jit(solution)/shard_map/ppermute | solution.py:529
  373.5 3.5 collective-permute-done.52
  378.2 6.4 %collective-permute-done.49 = bf16[4,32,1536]{2,1,0:T(8,128)(2,1)S(1)} collective-permute-done((bf16[4,32,1536]{2,1,0:T(8,128)(2,1)S(1)}, bf16[4,32,1536]{2,1,0:T(8,128)(2,1)S(1)}, u32[]{:S(2)}, u32[]{:S(2)}) %collective-permute-start.49) | collective-permute-done | bytes 393248 | tf_op jit(solution)/shard_map/ppermute | solution.py:529
  384.8 2.7 collective-permute-done.53
  387.8 3.2 collective-permute-start.56
  392.2 1.9 copy.83
  394.1 3.5 all-to-all-start.1
  397.6 2.9 collective-permute-start.54
  400.4 4.3 collective-permute-done.56
  408.8 2.5 copy.82
  411.3 3.7 all-to-all-start.2
  415.6 2.1 convert_bitcast_fusion
  418.6 4.3 add_convert_fusion.2
  422.9 7.4 %all-to-all-done.2 = bf16[8,4,32,512]{3,2,1,0:T(8,128)(2,1)S(1)} async-done(((bf16[8,4,32,512]{3,2,1,0:T(8,128)(2,1)}), bf16[8,4,32,512]{3,2,1,0:T(8,128)(2,1)S(1)}, u32[]{:S(2)}, u32[]{:S(2)}) %all-to-all-start.2) | async-done | bytes 1048608 | tf_op jit(solution)/shard_map/all_to_all | solution.py:729
  (272 shorter events, 53.9 us)
Async XLA Ops:
  9.9 28.3 %all-to-all-start = ((bf16[8,2,3,32,512]{4,3,2,1,0:T(8,128)(2,1)}), bf16[8,2,3,32,512]{4,3,2,1,0:T(8,128)(2,1)S(1)}, u32[]{:S(2)}, u32[]{:S(2)}) async-start(bf16[8,2,3,32,512]{4,3,2,1,0:T(8,128)(2,1)} %pad_maximum_fusion), calls=%async_computation | async-start | bytes 3145728 | tf_op jit(solution)/shard_map/all_to_all | solution.py:621
  15.2 142.5 %all-gather.2.cloned.1.call-start = ((), (), s32[]{:S(2)}) async-start(), calls=%async_computation.5 | async-start | bytes 7864320 | tf_op jit(solution)/shard_map/all_gather | solution.py:626
  20.1 18.0 %collective-permute-start.1 = (bf16[32,3200]{1,0:T(8,128)(2,1)S(1)}, bf16[32,3200]{1,0:T(8,128)(2,1)S(1)}, u32[]{:S(2)}, u32[]{:S(2)}) collective-permute-start(bf16[32,3200]{1,0:T(8,128)(2,1)S(1)} %concatenate.26), channel_id=1, source_target_pairs={{0,16},{1,17},{2,18},{3,19},{4,20},{5,21},{6,22},{7,23},{8,24},{9,... | collective-permute-start | bytes 614408 | tf_op jit(solution)/shard_map/ppermute | solution.py:529
  20.2 18.0 %collective-permute-start = (bf16[32,3200]{1,0:T(8,128)(2,1)S(1)}, bf16[32,3200]{1,0:T(8,128)(2,1)S(1)}, u32[]{:S(2)}, u32[]{:S(2)}) collective-permute-start(bf16[32,3200]{1,0:T(8,128)(2,1)S(1)} %concatenate.26), channel_id=1, source_target_pairs={{0,8},{1,9},{2,10},{3,11},{4,12},{5,13},{6,14},{7,15},{8,0},{9,1},... | collective-permute-start | bytes 614408 | tf_op jit(solution)/shard_map/ppermute | solution.py:529
  39.5 352.7 %reduce-scatter.5.cloned.1.call-start = ((), (), s32[]{:S(2)}) async-start(), calls=%async_computation.7 | async-start | bytes 2621440 | tf_op jit(solution)/shard_map/reduce_scatter | solution.py:674
  40.2 12.8 %collective-permute-start.7 = (bf16[4,32,1664]{2,1,0:T(8,128)(2,1)S(1)}, bf16[4,32,1664]{2,1,0:T(8,128)(2,1)S(1)}, u32[]{:S(2)}, u32[]{:S(2)}) collective-permute-start(bf16[4,32,1664]{2,1,0:T(8,128)(2,1)S(1)} %pad_maximum_fusion.4.refs_4_), channel_id=1, source_target_pairs={{0,4},{1,5},{2,6},{3,7},{4,0},{5,1},{6,2},{7,3},{8,12},{9,13},{10,... | collective-permute-start | bytes 1277960 | tf_op jit(solution)/shard_map/ppermute | solution.py:529
  42.1 17.9 %collective-permute-start.4 = (bf16[4,32,1536]{2,1,0:T(8,128)(2,1)S(1)}, bf16[4,32,1536]{2,1,0:T(8,128)(2,1)S(1)}, u32[]{:S(2)}, u32[]{:S(2)}) collective-permute-start(bf16[4,32,1536]{2,1,0:T(8,128)(2,1)S(1)} %pad_maximum_fusion.5.refs_0_), channel_id=1, source_target_pairs={{0,4},{1,5},{2,6},{3,7},{4,0},{5,1},{6,2},{7,3},{8,12},{9,13},{10,... | collective-permute-start | bytes 1179656 | tf_op jit(solution)/shard_map/ppermute | solution.py:529
  42.5 17.5 %collective-permute-start.3 = (bf16[4,32,1536]{2,1,0:T(8,128)(2,1)S(1)}, bf16[4,32,1536]{2,1,0:T(8,128)(2,1)S(1)}, u32[]{:S(2)}, u32[]{:S(2)}) collective-permute-start(bf16[4,32,1536]{2,1,0:T(8,128)(2,1)S(1)} %pad_maximum_fusion.5.refs_0_), channel_id=1, source_target_pairs={{0,2},{1,3},{2,0},{3,1},{4,6},{5,7},{6,4},{7,5},{8,10},{9,11},{10,... | collective-permute-start | bytes 1179656 | tf_op jit(solution)/shard_map/ppermute | solution.py:529
  44.2 17.3 %collective-permute-start.13 = (bf16[4,32,1664]{2,1,0:T(8,128)(2,1)S(1)}, bf16[4,32,1664]{2,1,0:T(8,128)(2,1)S(1)}, u32[]{:S(2)}, u32[]{:S(2)}) collective-permute-start(bf16[4,32,1664]{2,1,0:T(8,128)(2,1)S(1)} %pad_maximum_fusion.4.refs_4_), channel_id=1, source_target_pairs={{0,1},{1,0},{2,3},{3,2},{4,5},{5,4},{6,7},{7,6},{8,9},{9,8},{10,11... | collective-permute-start | bytes 1277960 | tf_op jit(solution)/shard_map/ppermute | solution.py:529
  44.2 19.4 %collective-permute-start.6 = (bf16[4,32,1664]{2,1,0:T(8,128)(2,1)S(1)}, bf16[4,32,1664]{2,1,0:T(8,128)(2,1)S(1)}, u32[]{:S(2)}, u32[]{:S(2)}) collective-permute-start(bf16[4,32,1664]{2,1,0:T(8,128)(2,1)S(1)} %pad_maximum_fusion.4.refs_4_), channel_id=1, source_target_pairs={{0,2},{1,3},{2,0},{3,1},{4,6},{5,7},{6,4},{7,5},{8,10},{9,11},{10,... | collective-permute-start | bytes 1277960 | tf_op jit(solution)/shard_map/ppermute | solution.py:529
  52.9 19.0 %collective-permute-start.8 = (bf16[4,32,1664]{2,1,0:T(8,128)(2,1)S(1)}, bf16[4,32,1664]{2,1,0:T(8,128)(2,1)S(1)}, u32[]{:S(2)}, u32[]{:S(2)}) collective-permute-start(bf16[4,32,1664]{2,1,0:T(8,128)(2,1)S(1)} %collective-permute-done.7.refs_6_), channel_id=1, source_target_pairs={{0,2},{1,3},{2,0},{3,1},{4,6},{5,7},{6,4},{7,5},{8,10},{9,11},{10,... | collective-permute-start | bytes 1277960 | tf_op jit(solution)/shard_map/ppermute | solution.py:529
  60.1 12.4 %collective-permute-start.5 = (bf16[4,32,1536]{2,1,0:T(8,128)(2,1)S(1)}, bf16[4,32,1536]{2,1,0:T(8,128)(2,1)S(1)}, u32[]{:S(2)}, u32[]{:S(2)}) collective-permute-start(bf16[4,32,1536]{2,1,0:T(8,128)(2,1)S(1)} %collective-permute-done.3.refs_1_), channel_id=1, source_target_pairs={{0,4},{1,5},{2,6},{3,7},{4,0},{5,1},{6,2},{7,3},{8,12},{9,13},{10,... | collective-permute-start | bytes 1179656 | tf_op jit(solution)/shard_map/ppermute | solution.py:529
  61.4 12.9 %collective-permute-start.15 = (bf16[4,32,1664]{2,1,0:T(8,128)(2,1)S(1)}, bf16[4,32,1664]{2,1,0:T(8,128)(2,1)S(1)}, u32[]{:S(2)}, u32[]{:S(2)}) collective-permute-start(bf16[4,32,1664]{2,1,0:T(8,128)(2,1)S(1)} %collective-permute-done.7.refs_6_), channel_id=1, source_target_pairs={{0,1},{1,0},{2,3},{3,2},{4,5},{5,4},{6,7},{7,6},{8,9},{9,8},{10,11... | collective-permute-start | bytes 1277960 | tf_op jit(solution)/shard_map/ppermute | solution.py:529
  74.9 26.0 %collective-permute-start.18 = (bf16[512,1024]{1,0:T(8,128)(2,1)S(1)}, bf16[512,1024]{1,0:T(8,128)(2,1)S(1)}, u32[]{:S(2)}, u32[]{:S(2)}) collective-permute-start(bf16[512,1024]{1,0:T(8,128)(2,1)S(1)} %copy-done.1), channel_id=1, source_target_pairs={{0,4},{1,5},{2,6},{3,7},{4,0},{5,1},{6,2},{7,3},{8,12},{9,13},{10,... | collective-permute-start | bytes 3145736 | tf_op jit(solution)/shard_map/ppermute | solution.py:529
  76.7 24.9 %collective-permute-start.17 = (bf16[512,1024]{1,0:T(8,128)(2,1)S(1)}, bf16[512,1024]{1,0:T(8,128)(2,1)S(1)}, u32[]{:S(2)}, u32[]{:S(2)}) collective-permute-start(bf16[512,1024]{1,0:T(8,128)(2,1)S(1)} %copy-done.1), channel_id=1, source_target_pairs={{0,2},{1,3},{2,0},{3,1},{4,6},{5,7},{6,4},{7,5},{8,10},{9,11},{10,... | collective-permute-start | bytes 3145736 | tf_op jit(solution)/shard_map/ppermute | solution.py:529
  101.6 26.5 %collective-permute-start.20 = (bf16[528,1024]{1,0:T(8,128)(2,1)}, bf16[528,1024]{1,0:T(8,128)(2,1)S(1)}, u32[]{:S(2)}, u32[]{:S(2)}) collective-permute-start(bf16[528,1024]{1,0:T(8,128)(2,1)} %get-tuple-element.167.refs_0_.h2_ref), channel_id=1, source_target_pairs={{0,4},{1,5},{2,6},{3,7},{4,0},{5,1},{6,2},{7,3},{8,12},{9,13},{10,... | collective-permute-start | bytes 3244040 | tf_op jit(solution)/shard_map/ppermute | solution.py:529
  102.0 26.2 %collective-permute-start.19 = (bf16[528,1024]{1,0:T(8,128)(2,1)}, bf16[528,1024]{1,0:T(8,128)(2,1)S(1)}, u32[]{:S(2)}, u32[]{:S(2)}) collective-permute-start(bf16[528,1024]{1,0:T(8,128)(2,1)} %get-tuple-element.167.refs_0_.h2_ref), channel_id=1, source_target_pairs={{0,2},{1,3},{2,0},{3,1},{4,6},{5,7},{6,4},{7,5},{8,10},{9,11},{10,... | collective-permute-start | bytes 3244040 | tf_op jit(solution)/shard_map/ppermute | solution.py:529
  128.3 24.9 %collective-permute-start.25 = (bf16[512,1024]{1,0:T(8,128)(2,1)S(1)}, bf16[512,1024]{1,0:T(8,128)(2,1)S(1)}, u32[]{:S(2)}, u32[]{:S(2)}) collective-permute-start(bf16[512,1024]{1,0:T(8,128)(2,1)S(1)} %pad_maximum_fusion.3), channel_id=1, source_target_pairs={{0,2},{1,3},{2,0},{3,1},{4,6},{5,7},{6,4},{7,5},{8,10},{9,11},{10,... | collective-permute-start | bytes 3145736 | tf_op jit(solution)/shard_map/ppermute | solution.py:529
  130.2 25.7 %collective-permute-start.26 = (bf16[528,1024]{1,0:T(8,128)(2,1)S(1)}, bf16[528,1024]{1,0:T(8,128)(2,1)}, u32[]{:S(2)}, u32[]{:S(2)}) collective-permute-start(bf16[528,1024]{1,0:T(8,128)(2,1)S(1)} %pad_maximum_fusion.2), channel_id=1, source_target_pairs={{0,4},{1,5},{2,6},{3,7},{4,0},{5,1},{6,2},{7,3},{8,12},{9,13},{10,... | collective-permute-start | bytes 3244040 | tf_op jit(solution)/shard_map/ppermute | solution.py:529
  131.7 24.2 %collective-permute-start.23 = (bf16[528,1024]{1,0:T(8,128)(2,1)S(1)}, bf16[528,1024]{1,0:T(8,128)(2,1)S(1)}, u32[]{:S(2)}, u32[]{:S(2)}) collective-permute-start(bf16[528,1024]{1,0:T(8,128)(2,1)S(1)} %collective-permute-done.20.refs_0_), channel_id=1, source_target_pairs={{0,1},{1,0},{2,3},{3,2},{4,5},{5,4},{6,7},{7,6},{8,9},{9,8},{10,11... | collective-permute-start | bytes 3244040 | tf_op jit(solution)/shard_map/ppermute | solution.py:529
  131.8 24.2 %collective-permute-start.27 = (bf16[528,1024]{1,0:T(8,128)(2,1)S(1)}, bf16[528,1024]{1,0:T(8,128)(2,1)S(1)}, u32[]{:S(2)}, u32[]{:S(2)}) collective-permute-start(bf16[528,1024]{1,0:T(8,128)(2,1)S(1)} %collective-permute-done.19.refs_2_), channel_id=1, source_target_pairs={{0,1},{1,0},{2,3},{3,2},{4,5},{5,4},{6,7},{7,6},{8,9},{9,8},{10,11... | collective-permute-start | bytes 3244040 | tf_op jit(solution)/shard_map/ppermute | solution.py:529
  132.3 21.0 %collective-permute-start.24 = (bf16[512,1024]{1,0:T(8,128)(2,1)S(1)}, bf16[512,1024]{1,0:T(8,128)(2,1)S(1)}, u32[]{:S(2)}, u32[]{:S(2)}) collective-permute-start(bf16[512,1024]{1,0:T(8,128)(2,1)S(1)} %collective-permute-done.18.refs_2_), channel_id=1, source_target_pairs={{0,1},{1,0},{2,3},{3,2},{4,5},{5,4},{6,7},{7,6},{8,9},{9,8},{10,11... | collective-permute-start | bytes 3145736 | tf_op jit(solution)/shard_map/ppermute | solution.py:529
  157.0 23.2 %collective-permute-start.30 = (bf16[528,1024]{1,0:T(8,128)(2,1)}, bf16[528,1024]{1,0:T(8,128)(2,1)S(1)}, u32[]{:S(2)}, u32[]{:S(2)}) collective-permute-start(bf16[528,1024]{1,0:T(8,128)(2,1)} %collective-permute-done.26.refs_6_), channel_id=1, source_target_pairs={{0,1},{1,0},{2,3},{3,2},{4,5},{5,4},{6,7},{7,6},{8,9},{9,8},{10,11... | collective-permute-start | bytes 3244040 | tf_op jit(solution)/shard_map/ppermute | solution.py:529
  157.6 22.6 %collective-permute-start.29 = (bf16[512,1024]{1,0:T(8,128)(2,1)S(1)}, bf16[512,1024]{1,0:T(8,128)(2,1)}, u32[]{:S(2)}, u32[]{:S(2)}) collective-permute-start(bf16[512,1024]{1,0:T(8,128)(2,1)S(1)} %collective-permute-done.25.refs_4_), channel_id=1, source_target_pairs={{0,1},{1,0},{2,3},{3,2},{4,5},{5,4},{6,7},{7,6},{8,9},{9,8},{10,11... | collective-permute-start | bytes 3145736 | tf_op jit(solution)/shard_map/ppermute | solution.py:529
  217.6 14.3 %collective-permute-start.31 = (bf16[528,1024]{1,0:T(8,128)(2,1)}, bf16[528,1024]{1,0:T(8,128)(2,1)S(1)}, u32[]{:S(2)}, u32[]{:S(2)}) collective-permute-start(bf16[528,1024]{1,0:T(8,128)(2,1)} %get-tuple-element.199), channel_id=1, source_target_pairs={{0,1},{1,0},{2,3},{3,2},{4,5},{5,4},{6,7},{7,6},{8,9},{9,8},{10,11... | collective-permute-start | bytes 3244040 | tf_op jit(solution)/shard_map/ppermute | solution.py:529
  218.0 13.9 %collective-permute-start.32 = (bf16[528,1024]{1,0:T(8,128)(2,1)}, bf16[528,1024]{1,0:T(8,128)(2,1)S(1)}, u32[]{:S(2)}, u32[]{:S(2)}) collective-permute-start(bf16[528,1024]{1,0:T(8,128)(2,1)} %get-tuple-element.201), channel_id=1, source_target_pairs={{0,1},{1,0},{2,3},{3,2},{4,5},{5,4},{6,7},{7,6},{8,9},{9,8},{10,11... | collective-permute-start | bytes 3244040 | tf_op jit(solution)/shard_map/ppermute | solution.py:529
  234.4 17.6 %collective-permute-start.34 = (bf16[528,1024]{1,0:T(8,128)(2,1)}, bf16[528,1024]{1,0:T(8,128)(2,1)S(1)}, u32[]{:S(2)}, u32[]{:S(2)}) collective-permute-start(bf16[528,1024]{1,0:T(8,128)(2,1)} %get-tuple-element.215), channel_id=1, source_target_pairs={{0,1},{1,0},{2,3},{3,2},{4,5},{5,4},{6,7},{7,6},{8,9},{9,8},{10,11... | collective-permute-start | bytes 3244040 | tf_op jit(solution)/shard_map/ppermute | solution.py:529
  234.8 17.2 %collective-permute-start.35 = (bf16[528,1024]{1,0:T(8,128)(2,1)}, bf16[528,1024]{1,0:T(8,128)(2,1)}, u32[]{:S(2)}, u32[]{:S(2)}) collective-permute-start(bf16[528,1024]{1,0:T(8,128)(2,1)} %get-tuple-element.216), channel_id=1, source_target_pairs={{0,1},{1,0},{2,3},{3,2},{4,5},{5,4},{6,7},{7,6},{8,9},{9,8},{10,11... | collective-permute-start | bytes 3244040 | tf_op jit(solution)/shard_map/ppermute | solution.py:529
  234.9 17.1 %collective-permute-start.33 = (bf16[256,1024]{1,0:T(8,128)(2,1)}, bf16[256,1024]{1,0:T(8,128)(2,1)}, u32[]{:S(2)}, u32[]{:S(2)}) collective-permute-start(bf16[256,1024]{1,0:T(8,128)(2,1)} %add_convert_fusion.12), channel_id=1, source_target_pairs={{0,6},{1,7},{2,4},{3,5},{4,2},{5,3},{6,0},{7,1},{8,14},{9,15},{10,... | collective-permute-start | bytes 1572872 | tf_op jit(solution)/shard_map/ppermute | solution.py:529
  252.0 156.7 %reduce-scatter.3.cloned.1.call-start = ((), (), s32[]{:S(2)}) async-start(), calls=%async_computation.6 | async-start | bytes 5242880 | tf_op jit(solution)/shard_map/reduce_scatter | solution.py:674
  256.2 15.7 %collective-permute-start.36 = (bf16[272,1024]{1,0:T(8,128)(2,1)}, bf16[272,1024]{1,0:T(8,128)(2,1)S(1)}, u32[]{:S(2)}, u32[]{:S(2)}) collective-permute-start(bf16[272,1024]{1,0:T(8,128)(2,1)} %add_convert_fusion.9), channel_id=1, source_target_pairs={{0,6},{1,7},{2,4},{3,5},{4,2},{5,3},{6,0},{7,1},{8,14},{9,15},{10,... | collective-permute-start | bytes 1671176 | tf_op jit(solution)/shard_map/ppermute | solution.py:529
  272.0 29.6 %collective-permute-start.37 = (bf16[528,1024]{1,0:T(8,128)(2,1)}, bf16[528,1024]{1,0:T(8,128)(2,1)S(1)}, u32[]{:S(2)}, u32[]{:S(2)}) collective-permute-start(bf16[528,1024]{1,0:T(8,128)(2,1)} %add_convert_fusion), channel_id=1, source_target_pairs={{0,2},{1,3},{2,0},{3,1},{4,6},{5,7},{6,4},{7,5},{8,10},{9,11},{10,... | collective-permute-start | bytes 3244040 | tf_op jit(solution)/shard_map/ppermute | solution.py:529
  273.0 28.6 %collective-permute-start.38 = (bf16[528,1024]{1,0:T(8,128)(2,1)S(1)}, bf16[528,1024]{1,0:T(8,128)(2,1)S(1)}, u32[]{:S(2)}, u32[]{:S(2)}) collective-permute-start(bf16[528,1024]{1,0:T(8,128)(2,1)S(1)} %add_convert_fusion.1), channel_id=1, source_target_pairs={{0,4},{1,5},{2,6},{3,7},{4,0},{5,1},{6,2},{7,3},{8,12},{9,13},{10,... | collective-permute-start | bytes 3244040 | tf_op jit(solution)/shard_map/ppermute | solution.py:529
  274.4 27.2 %collective-permute-start.40 = (bf16[512,1024]{1,0:T(8,128)(2,1)}, bf16[512,1024]{1,0:T(8,128)(2,1)}, u32[]{:S(2)}, u32[]{:S(2)}) collective-permute-start(bf16[512,1024]{1,0:T(8,128)(2,1)} %get-tuple-element.243), channel_id=1, source_target_pairs={{0,1},{1,0},{2,3},{3,2},{4,5},{5,4},{6,7},{7,6},{8,9},{9,8},{10,11... | collective-permute-start | bytes 3145736 | tf_op jit(solution)/shard_map/ppermute | solution.py:529
  274.4 27.2 %collective-permute-start.41 = (bf16[512,1024]{1,0:T(8,128)(2,1)}, bf16[512,1024]{1,0:T(8,128)(2,1)}, u32[]{:S(2)}, u32[]{:S(2)}) collective-permute-start(bf16[512,1024]{1,0:T(8,128)(2,1)} %get-tuple-element.245), channel_id=1, source_target_pairs={{0,1},{1,0},{2,3},{3,2},{4,5},{5,4},{6,7},{7,6},{8,9},{9,8},{10,11... | collective-permute-start | bytes 3145736 | tf_op jit(solution)/shard_map/ppermute | solution.py:529
  275.0 26.6 %collective-permute-start.42 = (bf16[512,1024]{1,0:T(8,128)(2,1)}, bf16[512,1024]{1,0:T(8,128)(2,1)}, u32[]{:S(2)}, u32[]{:S(2)}) collective-permute-start(bf16[512,1024]{1,0:T(8,128)(2,1)} %get-tuple-element.247), channel_id=1, source_target_pairs={{0,1},{1,0},{2,3},{3,2},{4,5},{5,4},{6,7},{7,6},{8,9},{9,8},{10,11... | collective-permute-start | bytes 3145736 | tf_op jit(solution)/shard_map/ppermute | solution.py:529
  310.9 37.9 %collective-permute-start.43 = (bf16[512,1024]{1,0:T(8,128)(2,1)}, bf16[512,1024]{1,0:T(8,128)(2,1)S(1)}, u32[]{:S(2)}, u32[]{:S(2)}) collective-permute-start(bf16[512,1024]{1,0:T(8,128)(2,1)} %add_convert_fusion.4), channel_id=1, source_target_pairs={{0,2},{1,3},{2,0},{3,1},{4,6},{5,7},{6,4},{7,5},{8,10},{9,11},{10,... | collective-permute-start | bytes 3145736 | tf_op jit(solution)/shard_map/ppermute | solution.py:529
  311.9 36.9 %collective-permute-start.44 = (bf16[512,1024]{1,0:T(8,128)(2,1)S(1)}, bf16[512,1024]{1,0:T(8,128)(2,1)S(1)}, u32[]{:S(2)}, u32[]{:S(2)}) collective-permute-start(bf16[512,1024]{1,0:T(8,128)(2,1)S(1)} %add_convert_fusion.3), channel_id=1, source_target_pairs={{0,4},{1,5},{2,6},{3,7},{4,0},{5,1},{6,2},{7,3},{8,12},{9,13},{10,... | collective-permute-start | bytes 3145736 | tf_op jit(solution)/shard_map/ppermute | solution.py:529
  313.3 35.4 %collective-permute-start.45 = (bf16[256,1024]{1,0:T(8,128)(2,1)}, bf16[256,1024]{1,0:T(8,128)(2,1)S(1)}, u32[]{:S(2)}, u32[]{:S(2)}) collective-permute-start(bf16[256,1024]{1,0:T(8,128)(2,1)} %get-tuple-element.286), channel_id=1, source_target_pairs={{0,6},{1,7},{2,4},{3,5},{4,2},{5,3},{6,0},{7,1},{8,14},{9,15},{10,... | collective-permute-start | bytes 1572872 | tf_op jit(solution)/shard_map/ppermute | solution.py:529
  352.7 19.6 %collective-permute-start.48 = (bf16[8,32,1536]{2,1,0:T(8,128)(2,1)S(1)}, bf16[8,32,1536]{2,1,0:T(8,128)(2,1)S(1)}, u32[]{:S(2)}, u32[]{:S(2)}) collective-permute-start(bf16[8,32,1536]{2,1,0:T(8,128)(2,1)S(1)} %add_convert_fusion.7), channel_id=1, source_target_pairs={{0,2},{1,3},{2,0},{3,1},{4,6},{5,7},{6,4},{7,5},{8,10},{9,11},{10,... | collective-permute-start | bytes 2359304 | tf_op jit(solution)/shard_map/ppermute | solution.py:529
  355.2 21.9 %collective-permute-start.52 = (bf16[8,32,1664]{2,1,0:T(8,128)(2,1)S(1)}, bf16[8,32,1664]{2,1,0:T(8,128)(2,1)S(1)}, u32[]{:S(2)}, u32[]{:S(2)}) collective-permute-start(bf16[8,32,1664]{2,1,0:T(8,128)(2,1)S(1)} %add_convert_fusion.5), channel_id=1, source_target_pairs={{0,4},{1,5},{2,6},{3,7},{4,0},{5,1},{6,2},{7,3},{8,12},{9,13},{10,... | collective-permute-start | bytes 2555912 | tf_op jit(solution)/shard_map/ppermute | solution.py:529
  372.5 12.2 %collective-permute-start.49 = (bf16[4,32,1536]{2,1,0:T(8,128)(2,1)S(1)}, bf16[4,32,1536]{2,1,0:T(8,128)(2,1)S(1)}, u32[]{:S(2)}, u32[]{:S(2)}) collective-permute-start(bf16[4,32,1536]{2,1,0:T(8,128)(2,1)S(1)} %add_convert_fusion.17), channel_id=1, source_target_pairs={{0,4},{1,5},{2,6},{3,7},{4,0},{5,1},{6,2},{7,3},{8,12},{9,13},{10,... | collective-permute-start | bytes 1179656 | tf_op jit(solution)/shard_map/ppermute | solution.py:529
  387.7 12.7 %collective-permute-start.55 = (bf16[32,3200]{1,0:T(8,128)(2,1)S(1)}, bf16[32,3200]{1,0:T(8,128)(2,1)S(1)}, u32[]{:S(2)}, u32[]{:S(2)}) collective-permute-start(bf16[32,3200]{1,0:T(8,128)(2,1)S(1)} %get-tuple-element.348), channel_id=1, source_target_pairs={{0,8},{1,9},{2,10},{3,11},{4,12},{5,13},{6,14},{7,15},{8,0},{9,1},... | collective-permute-start | bytes 614408 | tf_op jit(solution)/shard_map/ppermute | solution.py:529
  387.8 16.9 %collective-permute-start.56 = (bf16[32,3200]{1,0:T(8,128)(2,1)S(1)}, bf16[32,3200]{1,0:T(8,128)(2,1)S(1)}, u32[]{:S(2)}, u32[]{:S(2)}) collective-permute-start(bf16[32,3200]{1,0:T(8,128)(2,1)S(1)} %get-tuple-element.349), channel_id=1, source_target_pairs={{0,16},{1,17},{2,18},{3,19},{4,20},{5,21},{6,22},{7,23},{8,24},{9,... | collective-permute-start | bytes 614408 | tf_op jit(solution)/shard_map/ppermute | solution.py:529
  391.0 13.7 %collective-permute-start.57 = (bf16[32,3200]{1,0:T(8,128)(2,1)S(1)}, bf16[32,3200]{1,0:T(8,128)(2,1)S(1)}, u32[]{:S(2)}, u32[]{:S(2)}) collective-permute-start(bf16[32,3200]{1,0:T(8,128)(2,1)S(1)} %get-tuple-element.350), channel_id=1, source_target_pairs={{0,24},{1,25},{2,26},{3,27},{4,28},{5,29},{6,30},{7,31},{8,16},{9,... | collective-permute-start | bytes 614408 | tf_op jit(solution)/shard_map/ppermute | solution.py:529
  394.1 14.7 %all-to-all-start.1 = ((bf16[8,2,32,512]{3,2,1,0:T(8,128)(2,1)}), bf16[8,2,32,512]{3,2,1,0:T(8,128)(2,1)S(1)}, u32[]{:S(2)}, u32[]{:S(2)}) async-start(bf16[8,2,32,512]{3,2,1,0:T(8,128)(2,1)} %bitcast.65), calls=%async_computation.3 | async-start | bytes 1048576 | tf_op jit(solution)/shard_map/all_to_all | solution.py:729
  397.6 21.1 %collective-permute-start.54 = (bf16[256,1024]{1,0:T(8,128)(2,1)}, bf16[256,1024]{1,0:T(8,128)(2,1)}, u32[]{:S(2)}, u32[]{:S(2)}) collective-permute-start(bf16[256,1024]{1,0:T(8,128)(2,1)} %get-tuple-element.300), channel_id=1, source_target_pairs={{0,6},{1,7},{2,4},{3,5},{4,2},{5,3},{6,0},{7,1},{8,14},{9,15},{10,... | collective-permute-start | bytes 1572872 | tf_op jit(solution)/shard_map/ppermute | solution.py:529
  411.3 19.0 %all-to-all-start.2 = ((bf16[8,4,32,512]{3,2,1,0:T(8,128)(2,1)}), bf16[8,4,32,512]{3,2,1,0:T(8,128)(2,1)S(1)}, u32[]{:S(2)}, u32[]{:S(2)}) async-start(bf16[8,4,32,512]{3,2,1,0:T(8,128)(2,1)} %bitcast.70), calls=%async_computation.4 | async-start | bytes 2097152 | tf_op jit(solution)/shard_map/all_to_all | solution.py:729
  (72 other events, 695.5 us)
Sparse Core Ops, SparseCore 0:
  39.6 115.5 all-gather.1
  252.2 42.1 reduce-scatter.4
  301.8 76.5 reduce-scatter.2
